TPU v7x, 128 devices: a whole 4x4x4 slice. The times are simulated.
128 devices in a mesh: group: 4 (over z), ctx: 32 (over x, y, core).
Axes of the slice: x: 4, y: 4, z: 4, core: 2. Of those that a mesh axis runs over, the one named last changes fastest.
Arguments:
- hidden_states: bfloat16 [2, 32, 4096], P(None, 'group'), may hold values from -6 to 6
- key_values: bfloat16 [32, 16384, 1024], P('group', 'ctx'), may hold values from -128 to 128
- lengths: int32 [32], replicated, may hold values from 1 to 16384, as said below
- move_source: int32 [12], replicated, may hold values from 0 to 31, as said below
- move_target: int32 [12], replicated, may hold values from 0 to 31, as said below
- query_weight: bfloat16 [4096, 8192], P(None, 'ctx'), may hold values from -0.13125 to 0.13125
- keyval_weight: bfloat16 [4096, 1024], P(None, 'ctx'), may hold values from -0.09375 to 0.09375
- query_gain: bfloat16 [128], replicated, may hold values from 0.25 to 1.75
- key_gain: bfloat16 [128], replicated, may hold values from 0.25 to 1.75
- output_weight: bfloat16 [8192, 4096], P('ctx'), may hold values from -0.125 to 0.125
Outputs:
- attended: bfloat16 [2, 32, 4096], P(None, 'group', 'ctx')
Inputs may be any that keep to these rules, and one draw needn't show every extreme that they name: `lengths`: some row holds exactly 16384 cached tokens. move_source lists distinct slots and move_target lists the same set of slots in another order; for every ordered pair of different groups exactly 1 entries have the source slot in the first group and the target slot in the second; group of a slot is slot // 8; rows of unlisted slots keep their slot. `move_target`: see move_source.
All inputs are finite; a program needn't handle non-finite values.
Results may differ from a plain program's by a relative error of at most 0.021.
Values may be sent and summed in bfloat16 or wider, within the bound.
A program may use at most 128 MiB of HBM per device.

v0:
```python
import jax
import jax.numpy as jnp
from jax import lax
from jax.sharding import PartitionSpec as P

D = 4096
HEADS = 64
KV_HEADS = 4
HEAD_DIM = 128
ROWS_GRP = 8
MOVE = 1
STEPS = 2


eps = 1e-06
theta = 1000000.0
floor_value = -1e30


def merged_2(part, axis, combine):
    gathered = jax.tree.map(lambda a: lax.all_gather(a, axis), part)

    def take(source):
        return jax.tree.map(lambda a: lax.dynamic_index_in_dim(a, source, 0, False), gathered)

    return lax.fori_loop(
        1, lax.axis_size(axis), lambda source, state: combine(state, take(source)), take(0)
    )


def normed_rotated(values, gain_row, position):
    halfway = values.shape[-1] // 2
    scaled = (
        values
        * lax.rsqrt(jnp.mean(values * values, axis=-1, keepdims=True) + eps)
        * gain_row.astype(jnp.float32)
    )
    freqs = theta ** (-2.0 * jnp.arange(halfway, dtype=jnp.float32) / values.shape[-1])
    angles = position.astype(jnp.float32)[..., None, None] * freqs
    leading = scaled[..., :halfway]
    trailing = scaled[..., halfway:]
    cosine = jnp.cos(angles)
    sine_part = jnp.sin(angles)
    return jnp.concatenate(
        [leading * cosine - trailing * sine_part, trailing * cosine + leading * sine_part], axis=-1
    )


def block_terms(scores, usable):
    masked = jnp.where(usable, scores, floor_value)
    highest = jnp.max(masked, axis=-1)
    weights = jnp.where(usable, jnp.exp(masked - highest[..., None]), 0.0)
    return (highest, jnp.sum(weights, axis=-1), weights.astype(jnp.bfloat16))


def combine_parts(earlier, later):
    highest = jnp.maximum(earlier[0], later[0])
    early_scale = jnp.exp(earlier[0] - highest)
    late_scale = jnp.exp(later[0] - highest)
    totals = earlier[1] * early_scale + later[1] * late_scale
    sums = earlier[2] * early_scale[..., None] + later[2] * late_scale[..., None]
    return (highest, totals, sums)


def attend(queries, keyvals, row_cache, row_lengths, query_gain, key_gain, output_weight):
    ctx_index = lax.axis_index("ctx")
    local_heads = HEADS // lax.axis_size("ctx")
    head_start = ctx_index * local_heads
    rows_here = row_cache.shape[0]
    block_len = row_cache.shape[1]
    per_group = HEADS // KV_HEADS
    score_scale = HEAD_DIM ** (-0.5)
    positions = row_lengths[None, :] + jnp.arange(STEPS, dtype=jnp.int32)[:, None]
    query_rot = normed_rotated(
        queries.reshape(STEPS, rows_here, HEADS, HEAD_DIM).astype(jnp.float32),
        query_gain,
        positions,
    ).astype(jnp.bfloat16)
    split_kv = keyvals.reshape(STEPS, rows_here, 2, KV_HEADS, HEAD_DIM)
    new_keys = normed_rotated(split_kv[:, :, 0].astype(jnp.float32), key_gain, positions).astype(
        jnp.bfloat16
    )
    new_values = split_kv[:, :, 1]
    grouped = query_rot.reshape(STEPS, rows_here, KV_HEADS, per_group, HEAD_DIM)
    cache_keys = row_cache[:, :, : KV_HEADS * HEAD_DIM].reshape(
        rows_here, block_len, KV_HEADS, HEAD_DIM
    )
    cache_values = row_cache[:, :, KV_HEADS * HEAD_DIM :].reshape(
        rows_here, block_len, KV_HEADS, HEAD_DIM
    )
    scores = (
        jnp.einsum("srgjd,rpgd->srgjp", grouped, cache_keys, preferred_element_type=jnp.float32)
        * score_scale
    )
    places = ctx_index * block_len + jnp.arange(block_len, dtype=jnp.int32)
    usable = (places[None, :] < row_lengths[:, None])[None, :, None, None, :]
    highest, totals, weights = block_terms(scores, usable)
    sums = jnp.einsum(
        "srgjp,rpgd->srgjd", weights, cache_values, preferred_element_type=jnp.float32
    )
    new_scores = (
        jnp.einsum("srgjd,trgd->srgjt", grouped, new_keys, preferred_element_type=jnp.float32)
        * score_scale
    )
    causal = (jnp.arange(STEPS)[None, :] <= jnp.arange(STEPS)[:, None]).reshape(
        STEPS, 1, 1, 1, STEPS
    )
    new_high, new_total, new_weights = block_terms(new_scores, causal)
    new_sums = jnp.einsum(
        "srgjt,trgd->srgjd", new_weights, new_values, preferred_element_type=jnp.float32
    )
    merged = merged_2((highest, totals, sums), "ctx", combine_parts)
    merged_peak, full_totals, full_sums = combine_parts(merged, (new_high, new_total, new_sums))
    whole = (full_sums / full_totals[..., None]).reshape(STEPS, rows_here, HEADS, HEAD_DIM)
    mine = lax.dynamic_slice_in_dim(whole, head_start, local_heads, 2).astype(jnp.bfloat16)
    partial_out = jnp.dot(
        mine.reshape(STEPS * rows_here, local_heads * HEAD_DIM),
        output_weight,
        preferred_element_type=jnp.float32,
    )
    partial_out = partial_out.reshape(STEPS, rows_here, D)
    return lax.psum_scatter(partial_out, "ctx", scatter_dimension=2, tiled=True).astype(
        jnp.bfloat16
    )


def per_device(
    hidden_states,
    key_values,
    lengths,
    move_source,
    move_target,
    query_weight,
    keyval_weight,
    query_gain,
    key_gain,
    output_weight,
):
    groups = lax.axis_size("group")
    group_index = lax.axis_index("group")
    listed = move_source.shape[0]
    source_group = move_source // ROWS_GRP
    target_group = move_target // ROWS_GRP
    order_ids = jnp.arange(listed, dtype=jnp.int32)
    same_pair = (source_group[None, :] == source_group[:, None]) & (
        target_group[None, :] == target_group[:, None]
    )
    ranks = jnp.sum(same_pair & (order_ids[None, :] < order_ids[:, None]), axis=1)
    peer_ids = jnp.arange(groups, dtype=jnp.int32)[:, None, None]
    rank_ids = jnp.arange(MOVE, dtype=jnp.int32)[None, :, None]
    out_match = (source_group == group_index) & (target_group == peer_ids) & (ranks == rank_ids)
    send_slot = jnp.sum(jnp.where(out_match, move_source % ROWS_GRP, 0), axis=2)
    in_match = (source_group == peer_ids) & (target_group == group_index) & (ranks == rank_ids)
    land_slot = jnp.sum(jnp.where(in_match, move_target % ROWS_GRP, 0), axis=2)
    is_peer = jnp.arange(groups, dtype=jnp.int32)[:, None] != group_index
    land_index = jnp.where(is_peer, land_slot, ROWS_GRP).reshape(-1)
    slots_here = group_index * ROWS_GRP + jnp.arange(ROWS_GRP, dtype=jnp.int32)
    hits = move_target[None, :] == slots_here[:, None]
    moved_from = jnp.sum(jnp.where(hits, move_source[None, :], 0), axis=1)
    anchor_here = jnp.where(jnp.any(hits, axis=1), moved_from, slots_here)
    new_lengths = lengths[anchor_here]
    flat_hidden = hidden_states.reshape(STEPS * ROWS_GRP, D)
    query_part = (
        jnp.dot(flat_hidden, query_weight, preferred_element_type=jnp.float32)
        .astype(jnp.bfloat16)
        .reshape(STEPS, ROWS_GRP, -1)
    )
    keyval_part = (
        jnp.dot(flat_hidden, keyval_weight, preferred_element_type=jnp.float32)
        .astype(jnp.bfloat16)
        .reshape(STEPS, ROWS_GRP, -1)
    )
    queries, keyvals = (
        lax.all_gather(query_part, "ctx", axis=2, tiled=True),
        lax.all_gather(keyval_part, "ctx", axis=2, tiled=True),
    )
    moving = groups * MOVE
    outgoing = key_values[send_slot.reshape(-1)].reshape(
        groups, MOVE, key_values.shape[1], key_values.shape[2]
    )
    arrived = lax.all_to_all(outgoing, "group", split_axis=0, concat_axis=0, tiled=True)
    row_cache = key_values.at[land_index].set(
        arrived.reshape(moving, key_values.shape[1], key_values.shape[2]), mode="drop"
    )
    return attend(queries, keyvals, row_cache, new_lengths, query_gain, key_gain, output_weight)


def solution(mesh):
    in_specs = (
        P(None, "group", None),
        P("group", "ctx", None),
        P(),
        P(),
        P(),
        P(None, "ctx"),
        P(None, "ctx"),
        P(),
        P(),
        P("ctx", None),
    )
    out_specs = P(None, "group", "ctx")
    return jax.shard_map(
        per_device, mesh=mesh, in_specs=in_specs, out_specs=out_specs, check_vma=False
    )
```

profile of v0, /device:TPU:1, one launch (start us, length us, event | category | flops | bytes accessed | tf_op | source)
XLA Modules:
  0.0 344.0 jit_solution(12641936946111004969)
XLA Ops:
  6.5 7.7 %copy.205 = bf16[8,512,1024]{2,1,0:T(8,128)(2,1)} copy(bf16[8,512,1024]{2,1,0:T(8,128)(2,1)} %param.13) | data formatting | bytes 16777216
  14.7 6.2 %gather_fusion.1 = bf16[4,512,1024]{2,1,0:T(8,128)(2,1)} fusion(bf16[8,512,1024]{2,1,0:T(8,128)(2,1)} %copy.205, s32[1024]{0:T(1024)S(1)} %pad_clamp_fusion), kind=kCustom, calls=%fused_computation.1 | custom fusion | bytes 8388624 | tf_op jit(solution)/shard_map/gather | solution.py:178
  20.8 6.0 %all-to-all-start = ((bf16[4,1,512,1024]{3,2,1,0:T(8,128)(2,1)}), bf16[4,1,512,1024]{3,2,1,0:T(8,128)(2,1)}, u32[]{:S(2)}, u32[]{:S(2)}) async-start(bf16[4,1,512,1024]{3,2,1,0:T(8,128)(2,1)} %bitcast.139), calls=%async_computation | async-start | bytes 8388608 | tf_op jit(solution)/shard_map/all_to_all | solution.py:181
  27.9 2.0 fusion.16
  29.9 25.7 %all_gather.24 = bf16[2,8,8192]{2,1,0:T(8,128)(2,1)S(1)} all-gather(bf16[2,8,256]{2,1,0:T(8,128)(2,1)S(1)} %fusion.16), channel_id=1, replica_groups=mesh['group'=4,'ctx'=32] {'ctx'}, dimensions={2}, use_global_device_ids=true | all-gather | bytes 270336 | tf_op jit(solution)/shard_map/all_gather | solution.py:174
  56.6 19.2 %all-to-all-done = bf16[4,1,512,1024]{3,2,1,0:T(8,128)(2,1)} async-done(((bf16[4,1,512,1024]{3,2,1,0:T(8,128)(2,1)}), bf16[4,1,512,1024]{3,2,1,0:T(8,128)(2,1)}, u32[]{:S(2)}, u32[]{:S(2)}) %all-to-all-start) | async-done | bytes 4194336 | tf_op jit(solution)/shard_map/all_to_all | solution.py:181
  75.8 10.0 %scatter_fusion = bf16[8,512,1024]{2,1,0:T(8,128)(2,1)} fusion(bf16[8,512,1024]{2,1,0:T(8,128)(2,1)} %copy.205, s32[4]{0:T(128)S(1)} %fusion.48, bf16[4,512,1024]{2,1,0:T(8,128)(2,1)} %bitcast.11), kind=kCustom, calls=%fused_computation.2 | custom fusion | bytes 12582928 | tf_op jit(solution)/shard_map/scatter | solution.py:182
  85.7 5.7 %fusion.58 = (bf16[8,512,512]{2,1,0:T(8,128)(2,1)}, bf16[8,512,512]{2,1,0:T(8,128)(2,1)}) fusion(bf16[8,512,1024]{2,1,0:T(8,128)(2,1)} %scatter_fusion), kind=kLoop, calls=%fused_computation.131 | loop fusion | bytes 16777216 | tf_op jit(solution)/shard_map/slice | solution.py:88
  91.4 6.5 %copy.90 = bf16[8,512,512]{1,2,0:T(8,128)(2,1)} copy(bf16[8,512,512]{2,1,0:T(8,128)(2,1)} %get-tuple-element.251) | data formatting | bytes 8388608 | tf_op jit(solution)/shard_map/slice | solution.py:85
  97.9 6.5 %copy.96 = bf16[8,512,512]{1,2,0:T(8,128)(2,1)} copy(bf16[8,512,512]{2,1,0:T(8,128)(2,1)} %get-tuple-element.250) | data formatting | bytes 8388608 | tf_op jit(solution)/shard_map/slice | solution.py:88
  104.4 3.3 bitcast_reduce_fusion
  107.7 1.3 copy-done.2
  109.0 2.3 convolution_bitcast_fusion.1
  111.7 26.5 %all_gather.31 = bf16[2,8,1024]{1,0,2:T(2,128)(2,1)S(1)} all-gather(bf16[2,8,32]{1,0,2:T(2,128)(2,1)S(1)} %copy.104), channel_id=1, replica_groups=mesh['group'=4,'ctx'=32] {'ctx'}, dimensions={2}, use_global_device_ids=true | all-gather | bytes 33792 | tf_op jit(solution)/shard_map/all_gather | solution.py:175
  138.9 0.8 fusion.60
  140.0 2.3 fusion.10
  142.3 25.9 %all-gather.1 = f32[64,8,4,16]{3,1,2,0:T(8,128)S(1)} all-gather(f32[2,8,4,16]{3,1,2,0:T(8,128)S(1)} %copy.95), channel_id=3, replica_groups=mesh['group'=4,'ctx'=32] {'ctx'}, dimensions={0}, use_global_device_ids=true | all-gather | bytes 135168 | tf_op jit(solution)/shard_map/all_gather | solution.py:21
  168.2 23.6 %all-gather = f32[64,8,4,16]{3,1,2,0:T(8,128)S(1)} all-gather(f32[2,8,4,16]{3,1,2,0:T(8,128)S(1)} %copy.94), channel_id=2, replica_groups=mesh['group'=4,'ctx'=32] {'ctx'}, dimensions={0}, use_global_device_ids=true | all-gather | bytes 135168 | tf_op jit(solution)/shard_map/all_gather | solution.py:21
  191.8 1.0 copy-done.5
  192.8 1.1 slice.48
  193.9 71.6 %while.19 = (s32[]{:T(128)}, f32[2,8,4,16]{3,2,1,0:T(4,128)S(1)}, f32[2,8,4,16]{3,2,1,0:T(4,128)S(1)}, f32[2,8,4,16,128]{4,3,2,1,0:T(8,128)S(1)}, f32[32,2,8,4,1...) while((s32[]{:T(128)}, f32[2,8,4,16]{3,2,1,0:T(4,128)S(1)}, ...), condition=%wide.region_10.11_spmd, body=%wide.region_9.10_spmd.sunk | while | flops 399365 | bytes 1630359 | solution.py:26
  194.0 0.8 constant_dynamic-slice_fusion.7
  194.8 1.4 fusion.69
  196.3 0.8 constant_dynamic-slice_fusion.7
  197.1 1.4 fusion.69
  198.6 0.8 constant_dynamic-slice_fusion.7
  199.4 1.4 fusion.69
  200.9 0.8 constant_dynamic-slice_fusion.7
  201.7 1.4 fusion.69
  203.2 0.8 constant_dynamic-slice_fusion.7
  204.0 1.4 fusion.69
  205.5 0.8 constant_dynamic-slice_fusion.7
  206.4 1.4 fusion.69
  208.7 1.4 fusion.69
  211.0 1.4 fusion.69
  213.3 1.4 fusion.69
  215.6 1.4 fusion.69
  217.9 1.4 fusion.69
  220.2 1.4 fusion.69
  221.7 0.8 constant_dynamic-slice_fusion.7
  222.5 1.4 fusion.69
  224.8 1.4 fusion.69
  227.2 1.4 fusion.69
  228.6 0.8 constant_dynamic-slice_fusion.7
  229.5 1.4 fusion.69
  231.8 1.4 fusion.69
  234.1 1.4 fusion.69
  236.4 1.4 fusion.69
  238.7 1.4 fusion.69
  241.0 1.4 fusion.69
  243.3 1.4 fusion.69
  245.6 1.4 fusion.69
  247.1 0.8 constant_dynamic-slice_fusion.7
  248.0 1.4 fusion.69
  250.3 1.4 fusion.69
  252.6 1.4 fusion.69
  254.9 1.4 fusion.69
  257.2 1.4 fusion.69
  259.5 1.4 fusion.69
  261.8 1.4 fusion.69
  264.1 1.4 fusion.69
  266.5 1.1 fusion.5
  267.6 68.2 %reduce-scatter.2.cloned.1.call-done = f32[2,8,128]{2,1,0:T(8,128)} async-done(((f32[2,8,4096]{2,1,0:T(8,128)}), f32[2,8,128]{2,1,0:T(8,128)}) %reduce-scatter.2.cloned.1.call-update) | async-done | bytes 8208 | tf_op jit(solution)/shard_map/reduce_scatter | solution.py:122
  335.8 1.3 convert_element_type.63
  (133 shorter events, 23.5 us)
Async XLA Ops:
  6.5 260.0 %copy-start = (bf16[256,4096]{1,0:T(8,128)(2,1)S(1)}, bf16[256,4096]{1,0:T(8,128)(2,1)}, u32[]{:S(2)}) copy-start(bf16[256,4096]{1,0:T(8,128)(2,1)} %param.21) | copy-start | bytes 6291460
  6.5 7.7 %copy-start.8 = (s32[12]{0:T(128)S(1)}, s32[12]{0:T(128)}, u32[]{:S(2)}) copy-start(s32[12]{0:T(128)} %param.15) | copy-start | bytes 148
  6.5 7.7 %copy-start.9 = (s32[12]{0:T(128)S(1)}, s32[12]{0:T(128)}, u32[]{:S(2)}) copy-start(s32[12]{0:T(128)} %param.16) | copy-start | bytes 148
  20.8 6.0 %copy-start.10 = (bf16[128]{0:T(256)(128)(2,1)S(1)}, bf16[128]{0:T(256)(128)(2,1)}, u32[]{:S(2)}) copy-start(bf16[128]{0:T(256)(128)(2,1)} %param.19) | copy-start | bytes 772
  20.8 6.4 %copy-start.1 = (s32[32]{0:T(128)S(1)}, s32[32]{0:T(128)}, u32[]{:S(2)}) copy-start(s32[32]{0:T(128)} %param.14) | copy-start | bytes 388
  20.8 7.1 %copy-start.6 = (bf16[2,8,4096]{2,1,0:T(8,128)(2,1)S(1)}, bf16[2,8,4096]{2,1,0:T(8,128)(2,1)}, u32[]{:S(2)}) copy-start(bf16[2,8,4096]{2,1,0:T(8,128)(2,1)} %param.12) | copy-start | bytes 393220
  20.8 54.9 %all-to-all-start = ((bf16[4,1,512,1024]{3,2,1,0:T(8,128)(2,1)}), bf16[4,1,512,1024]{3,2,1,0:T(8,128)(2,1)}, u32[]{:S(2)}, u32[]{:S(2)}) async-start(bf16[4,1,512,1024]{3,2,1,0:T(8,128)(2,1)} %bitcast.139), calls=%async_computation | async-start | bytes 8388608 | tf_op jit(solution)/shard_map/all_to_all | solution.py:181
  26.8 166.0 %all-gather.5.cloned.1.call-start = ((), (), s32[]{:S(2)}) async-start(), calls=%async_computation.3 | async-start | bytes 17301504 | tf_op jit(solution)/shard_map/all_gather | solution.py:21
  104.4 4.6 %copy-start.3 = (bf16[8,512,512]{1,2,0:T(8,128)(2,1)S(1)}, bf16[8,512,512]{1,2,0:T(8,128)(2,1)}, u32[]{:S(2)}) copy-start(bf16[8,512,512]{1,2,0:T(8,128)(2,1)} %copy.96) | copy-start | bytes 12582916
  107.6 1.4 copy-start.2
  109.0 2.4 copy-start.7
  109.0 29.5 %copy-start.11 = (bf16[128]{0:T(256)(128)(2,1)S(1)}, bf16[128]{0:T(256)(128)(2,1)}, u32[]{:S(2)}) copy-start(bf16[128]{0:T(256)(128)(2,1)} %param.20) | copy-start | bytes 772
  111.4 224.5 %reduce-scatter.2.cloned.1.call-start = ((), (), s32[]{:S(2)}) async-start(), calls=%async_computation.2 | async-start | bytes 270336 | tf_op jit(solution)/shard_map/reduce_scatter | solution.py:122
  168.2 23.6 %copy-start.4 = (f32[64,8,4,16]{3,1,2,0:T(8,128)}, f32[64,8,4,16]{3,1,2,0:T(8,128)S(1)}, u32[]{:S(2)}) copy-start(f32[64,8,4,16]{3,1,2,0:T(8,128)S(1)} %all-gather.1) | copy-start | bytes 393220
  191.8 1.0 copy-start.5
Sparse Core Ops, SparseCore 0:
  111.5 77.5 all-gather.4
  267.7 68.0 reduce-scatter.1
where the time goes:
time: 350 us; the launch traced here: 344 us
  blocking collectives  102 us (29%)
  waiting for transfers between devices  87.4 us (25%)
  local copies, waits for them, and re-layouts  71.6 us (20%)
  other arithmetic  52.4 us (15%)
  between operations  13.8 us (4%)
  matrix products  10.4 us (3%)
  starting transfers between devices  6.03 us (2%)
    reduce_scatter x1, waiting for transfers between devices, attend(): lax.psum_scatter(partial_out, 'ctx', scatter_dimension=2, tiled=True)  68.2 us
    all_gather x2, blocking collectives, merged_2(): gathered = jax.tree.map(lambda a: lax.all_gather(a, axis), part)  49.4 us
    add x31, other arithmetic, combine_parts(): earlier[2] * early_scale[..., None] + later[2] * late_scale[..., None]  44.8 us
    all_gather x1, blocking collectives, per_device(): lax.all_gather(keyval_part, 'ctx', axis=2, tiled=True)  26.5 us
    all_gather x1, blocking collectives, per_device(): lax.all_gather(query_part, 'ctx', axis=2, tiled=True)  25.7 us
    dynamic_slice x34, local copies, waits for them, and re-layouts, take(): lax.dynamic_index_in_dim(a, source, 0, False)  25.4 us
    all_to_all x1, waiting for transfers between devices, per_device(): lax.all_to_all(outgoing, 'group', split_axis=0, concat_axis=0, tiled=True)  19.2 us
    slice x2, local copies, waits for them, and re-layouts, attend(): row_cache[:, :, KV_HEADS * HEAD_DIM:]  12.2 us
  transfers between devices with their start and end apart: 3, of which 2 were waited for; matrix products, arithmetic and copies ran while one was open for 2% of the time, Pallas kernels for 0%

commit v1 on v0

v1 whole, which is shorter than its diff:
```python
import functools
import math

import jax
import jax.numpy as jnp
import numpy as np
from jax import lax
from jax.experimental import pallas as pl
from jax.experimental.pallas import tpu as pltpu
from jax.sharding import PartitionSpec as P

MESH = pl.DeviceIdType.MESH
F32 = jnp.float32
BF16 = jnp.bfloat16

ROWS = 8
STEPS = 2
KV_HEADS = 4
HEAD_DIM = 128
LOCAL_HEADS = 2
Q = LOCAL_HEADS * STEPS
RQ = ROWS * Q
SR = STEPS * ROWS
EPS = 1e-6
THETA = 1000000.0
FLOOR = -1e30
LOW = -1e29
QSCALE = HEAD_DIM**-0.5 * math.log2(math.e)


def iota(shape, dim):
    return lax.broadcasted_iota(jnp.int32, shape, dim)


def normed(x, gain):
    return x * lax.rsqrt(jnp.mean(x * x, axis=-1, keepdims=True) + EPS) * gain


def rotated(x, cos, sin):
    return x * cos + pltpu.roll(x, HEAD_DIM // 2, 1) * sin


def kernel(
    G, C, D, BLK,
    hidden_h, cache_h, lengths_h, source_h, target_h, wq_h, wkv_h, qgain_h, kgain_h, wo_h, freq_h,
    out_ref,
    hidden, cache, wq, wkv, wo, qgain, kgain, freq, lengths, source, target,
    z_send, z_recv, q_all, kv_send, kv_recv, q_rows, a_send, a_recv, mix, o_send, o_recv, y_send, y_recv,
    load_sem, cache_sem, zs_sem, zr_sem, qs_sem, qr_sem, ks_sem, kr_sem, as_sem, ar_sem, os_sem, or_sem, ys_sem, yr_sem,
):
    JJ = C // KV_HEADS
    KVW = 2 * KV_HEADS * HEAD_DIM // C
    PIECES = HEAD_DIM // KVW
    my_g = lax.axis_index("group")
    my_c = lax.axis_index("ctx")
    my_x = my_c // JJ
    my_low = lax.rem(my_c, JJ)

    loads = [
        (hidden_h, hidden), (wkv_h, wkv), (wq_h, wq), (lengths_h, lengths), (source_h, source), (target_h, target),
        (freq_h, freq), (qgain_h, qgain), (kgain_h, kgain), (wo_h, wo),
    ]
    loads = [pltpu.make_async_copy(a, b, load_sem.at[n]) for n, (a, b) in enumerate(loads)]
    for load in loads[:-1]:
        load.start()
    cache_loads = [pltpu.make_async_copy(cache_h.at[r], cache.at[r], cache_sem.at[r]) for r in range(ROWS)]
    for load in cache_loads:
        load.start()
    loads[-1].start()

    barrier = pltpu.get_barrier_semaphore()

    def greet(n, carry):
        pl.semaphore_signal(
            barrier, inc=1, device_id={"ctx": lax.rem(my_c + n, C)}, device_id_type=MESH
        )
        return carry

    for n in range(1, G):
        pl.semaphore_signal(barrier, inc=1, device_id={"group": lax.rem(my_g + n, G)}, device_id_type=MESH)
    lax.fori_loop(1, C, greet, 0)

    for load in loads[3:9]:
        load.wait()
    row_id = iota((SR, HEAD_DIM), 0)
    lane_id = iota((SR, HEAD_DIM), 1)
    slot_id = lax.rem(row_id, ROWS)
    position = row_id // ROWS
    for r in range(ROWS):
        position = position + jnp.where(slot_id == r, lengths[my_g * ROWS + r], 0)
    angle = position.astype(F32) * freq[...]
    cos = jnp.cos(angle)
    sin = jnp.sin(angle)
    sin = jnp.where(lane_id < HEAD_DIM // 2, -sin, sin)
    q_gain = qgain[...].astype(F32).reshape(1, HEAD_DIM) * QSCALE
    k_gain = kgain[...].astype(F32).reshape(1, HEAD_DIM)

    entries = source.shape[0]

    def slots(peer):
        away = jnp.int32(0)
        home = jnp.int32(0)
        for e in range(entries):
            s, t = source[e], target[e]
            away = away + jnp.where((s // ROWS == my_g) & (t // ROWS == peer), lax.rem(s, ROWS), 0)
            home = home + jnp.where((s // ROWS == peer) & (t // ROWS == my_g), lax.rem(t, ROWS), 0)
        return away, home

    ahead = [slots(lax.rem(my_g + n, G)) for n in range(1, G)]
    behind = [slots(lax.rem(my_g + G - n, G)) for n in range(1, G)]

    for load in loads[:3]:
        load.wait()
    h = jnp.concatenate([hidden[0], hidden[1]], axis=0)
    kv = jnp.dot(h, wkv[...], preferred_element_type=F32).astype(BF16).astype(F32)
    kv = jnp.concatenate([kv] * PIECES, axis=1)
    q = jnp.dot(h, wq[...], preferred_element_type=F32).astype(BF16).astype(F32)
    heads = [q[:, j * HEAD_DIM : (j + 1) * HEAD_DIM] for j in range(LOCAL_HEADS)] + [kv]

    for n in range(G - 1):
        message = jnp.zeros((SR, HEAD_DIM), F32)
        for j, x in enumerate(heads):
            picked = jnp.where(slot_id == ahead[n][1], x, 0.0)
            for s in range(STEPS):
                line = jnp.sum(picked[s * ROWS : (s + 1) * ROWS], axis=0, keepdims=True)
                message = jnp.where(row_id == j * STEPS + s, line, message)
        z_send[n] = message.astype(BF16)

    pl.semaphore_wait(barrier, C - 1 + G - 1)

    z_copies = [
        pltpu.make_async_remote_copy(
            src_ref=z_send.at[n], dst_ref=z_recv.at[n], send_sem=zs_sem.at[n], recv_sem=zr_sem.at[n],
            device_id={"group": lax.rem(my_g + n + 1, G)}, device_id_type=MESH,
        )
        for n in range(G - 1)
    ]
    for copy in z_copies:
        copy.start()
    for copy in z_copies:
        copy.wait_recv()
    for n in range(G - 1):
        came = z_recv[n].astype(F32)
        for j in range(len(heads)):
            for s in range(STEPS):
                line = came[j * STEPS + s : j * STEPS + s + 1, :]
                heads[j] = jnp.where((slot_id == behind[n][0]) & (row_id // ROWS == s), line, heads[j])

    for j in range(LOCAL_HEADS):
        turned = rotated(normed(heads[j], q_gain), cos, sin)
        for s in range(STEPS):
            q_rows[pl.ds(j * STEPS + s, ROWS, stride=Q), :] = turned[s * ROWS : (s + 1) * ROWS]
    q_mine = q_rows[...].astype(BF16)
    q_all[my_c] = q_mine
    kv_send[...] = heads[LOCAL_HEADS].astype(BF16)

    def q_copy(dest):
        return pltpu.make_async_remote_copy(
            src_ref=q_all.at[my_c], dst_ref=q_all.at[my_c], send_sem=qs_sem, recv_sem=qr_sem.at[my_x],
            device_id={"ctx": dest}, device_id_type=MESH,
        )

    def send_q(n, carry):
        q_copy(lax.rem(my_x + KV_HEADS - n // JJ, KV_HEADS) * JJ + lax.rem(my_low + n, JJ)).start()
        return carry

    lax.fori_loop(1, C, send_q, 0)

    kv_head = lax.rem(my_c, C // 2) // PIECES
    kv_slot = my_c // (C // 2) * PIECES + lax.rem(my_c, PIECES)

    def kv_copy(dest):
        return pltpu.make_async_remote_copy(
            src_ref=kv_send, dst_ref=kv_recv.at[kv_slot], send_sem=ks_sem, recv_sem=kr_sem.at[kv_slot],
            device_id={"ctx": dest}, device_id_type=MESH,
        )

    def send_kv(n, carry):
        dest = kv_head * JJ + n

        @pl.when(dest != my_c)
        def _():
            kv_copy(dest).start()

        return carry

    lax.fori_loop(0, JJ, send_kv, 0)

    @pl.when(kv_head == my_x)
    def _():
        kv_recv[kv_slot] = kv_send[...]

    ALL = JJ * RQ
    pi, pj = iota((ALL, ALL), 0), iota((ALL, ALL), 1)
    to_rows = pj == lax.rem(pi // Q, JJ) * RQ + pi // (JJ * Q) * Q + lax.rem(pi, Q)
    to_devices = pj == lax.rem(pi // Q, ROWS) * (JJ * Q) + pi // RQ * Q + lax.rem(pi, Q)
    to_rows = to_rows.astype(F32).astype(BF16)
    to_devices = to_devices.astype(F32).astype(BF16)
    gi, gj = iota((JJ * 16, 2 * ALL), 0), iota((JJ * 16, 2 * ALL), 1)
    gather = (
        (lax.rem(gi // 8, 2) == gj // ALL)
        & (gi // 16 == lax.rem(gj // Q, JJ))
        & (lax.rem(gi, Q) == lax.rem(gj, Q))
        & (lax.rem(gi // Q, 2) == lax.rem(gj // (JJ * Q), 2))
    ).astype(F32).astype(BF16)

    place = iota((JJ * Q, BLK), 1) + my_c * BLK
    lanes = iota((JJ * Q, HEAD_DIM), 1)
    for load in cache_loads:
        load.wait()

    def a_copy(dest):
        return pltpu.make_async_remote_copy(
            src_ref=a_send.at[dest], dst_ref=a_recv.at[my_c], send_sem=as_sem, recv_sem=ar_sem,
            device_id={"ctx": dest}, device_id_type=MESH,
        )

    def one_head(i, carry):
        g = lax.rem(my_x + i, KV_HEADS)

        @pl.when(i == 0)
        def _():
            if JJ > 1:
                some = q_all.at[pl.ds(0, JJ - 1)]
                pltpu.make_async_copy(some, some, qr_sem.at[g]).wait()

        @pl.when(i > 0)
        def _():
            some = q_all.at[pl.ds(0, JJ)]
            pltpu.make_async_copy(some, some, qr_sem.at[g]).wait()

        came = q_all[pl.ds(g * JJ, JJ)].reshape(ALL, HEAD_DIM)
        queries = jnp.dot(to_rows, came, preferred_element_type=F32).astype(BF16)
        k_at = pl.ds(pl.multiple_of(g * HEAD_DIM, HEAD_DIM), HEAD_DIM)
        v_at = pl.ds(pl.multiple_of((g + KV_HEADS) * HEAD_DIM, HEAD_DIM), HEAD_DIM)
        sums, peaks, totals = [], [], []
        for r in range(ROWS):
            scores = lax.dot_general(
                queries[r * JJ * Q : (r + 1) * JJ * Q], cache[r, :, k_at], (((1,), (1,)), ((), ())),
                preferred_element_type=F32,
            )
            scores = jnp.where(place < lengths[my_g * ROWS + r], scores, FLOOR)
            peak = jnp.maximum(jnp.max(scores, axis=1, keepdims=True), LOW).astype(BF16).astype(F32)
            weights = jnp.exp2(scores - peak)
            total = jnp.sum(weights, axis=1, keepdims=True)
            a = jnp.dot(weights.astype(BF16), cache[r, :, v_at], preferred_element_type=F32)
            high = total.astype(BF16).astype(F32)
            sums.append(a.astype(BF16))
            peaks.append(jnp.where(lanes & 3 == r // 2, peak, 0.0).astype(BF16))
            totals.append(
                jnp.where(lanes == r // 2, high, jnp.where(lanes == 4 + r // 2, total - high, 0.0)).astype(BF16)
            )
        sums = jnp.dot(to_devices, jnp.concatenate(sums, axis=0), preferred_element_type=F32)
        stats = jnp.dot(gather, jnp.concatenate(peaks + totals, axis=0), preferred_element_type=F32)
        a_send[pl.ds(g * JJ, JJ), :RQ] = sums.astype(BF16).reshape(JJ, RQ, HEAD_DIM)
        a_send[pl.ds(g * JJ, JJ), RQ:] = stats.astype(BF16).reshape(JJ, 16, HEAD_DIM)

        def send_a(n, carry):
            a_copy(g * JJ + lax.rem(my_low + n, JJ)).start()
            return carry

        lax.fori_loop(jnp.where(i == 0, 1, 0), JJ, send_a, 0)
        return carry

    lax.fori_loop(0, KV_HEADS, one_head, 0)
    a_recv[my_c] = a_send[my_c]

    def get_kv(n, carry):
        @pl.when(n // PIECES * (C // 2) + my_x * PIECES + lax.rem(n, PIECES) != my_c)
        def _():
            pltpu.make_async_copy(kv_send, kv_recv.at[n], kr_sem.at[n]).wait()

        return carry

    lax.fori_loop(0, 2 * PIECES, get_kv, 0)
    new = []
    for kind in range(2):
        x = kv_recv[kind * PIECES].astype(F32)
        for n in range(1, PIECES):
            x = jnp.where(lane_id // KVW == n, kv_recv[kind * PIECES + n].astype(F32), x)
        new.append(x)
    new_key = rotated(normed(new[0], k_gain), cos, sin).astype(BF16)
    new_value = new[1].astype(BF16)
    scores = lax.dot_general(q_mine, new_key, (((1,), (1,)), ((), ())), preferred_element_type=F32)
    ti, tj = iota((RQ, SR), 0), iota((RQ, SR), 1)
    scores = jnp.where((ti // Q == lax.rem(tj, ROWS)) & (tj // ROWS <= lax.rem(ti, STEPS)), scores, FLOOR)
    peak = jnp.max(scores, axis=1, keepdims=True)
    weights = jnp.exp2(scores - peak)
    total = jnp.sum(weights, axis=1, keepdims=True)
    new_sums = jnp.dot(weights.astype(BF16), new_value, preferred_element_type=F32)
    ui, uj = iota((RQ, HEAD_DIM), 0), iota((RQ, HEAD_DIM), 1)
    peak = jnp.where(uj & 3 == ui // 8, peak, 0.0)
    total = jnp.where(uj == ui // 8, total, 0.0)
    peak = peak[0:8] + peak[8:16] + peak[16:24] + peak[24:32]
    total = total[0:8] + total[8:16] + total[16:24] + total[24:32]

    some = a_recv.at[pl.ds(0, C - 1)]
    pltpu.make_async_copy(some, some, ar_sem).wait()
    stats = a_recv[:, RQ:].astype(F32)
    peaks = stats[:, :8]
    highest = jnp.maximum(jnp.max(peaks, axis=0), peak)
    scale = jnp.exp2(peaks - highest[None])
    new_scale = jnp.exp2(peak - highest)
    norm = jnp.sum(scale * stats[:, 8:], axis=0) + new_scale * total
    arrived = a_recv[:, :RQ].astype(F32)
    for k in range(RQ // 8):
        rows = slice(k * 8, (k + 1) * 8)
        acc = jnp.sum(arrived[:, rows] * scale[:, :, k : k + 1], axis=0) + new_sums[rows] * new_scale[:, k : k + 1]
        mix[rows, :] = acc / (norm[:, k : k + 1] + norm[:, 4 + k : 5 + k])
    mixed = jnp.concatenate(
        [
            jnp.concatenate([mix[pl.ds(j * STEPS + s, ROWS, stride=Q), :] for s in range(STEPS)], axis=0)
            for j in range(LOCAL_HEADS)
        ],
        axis=1,
    ).astype(BF16)

    loads[-1].wait()
    quarter = D // KV_HEADS
    width = D // C

    def o_copy(dest):
        return pltpu.make_async_remote_copy(
            src_ref=o_send.at[dest], dst_ref=o_recv.at[my_c], send_sem=os_sem, recv_sem=or_sem,
            device_id={"ctx": dest}, device_id_type=MESH,
        )

    def one_quarter(i, carry):
        g = lax.rem(my_x + i, KV_HEADS)
        part = jnp.dot(
            mixed, wo[:, pl.ds(pl.multiple_of(g * quarter, quarter), quarter)], preferred_element_type=F32
        ).astype(BF16)
        for n in range(JJ):
            o_send[g * JJ + n] = part[:, n * width : (n + 1) * width]

        def send_o(n, carry):
            o_copy(g * JJ + lax.rem(my_low + n, JJ)).start()
            return carry

        lax.fori_loop(jnp.where(i == 0, 1, 0), JJ, send_o, 0)
        return carry

    lax.fori_loop(0, KV_HEADS, one_quarter, 0)
    o_recv[my_c] = o_send[my_c]
    some = o_recv.at[pl.ds(0, C - 1)]
    pltpu.make_async_copy(some, some, or_sem).wait()
    result = jnp.sum(o_recv[...].astype(F32), axis=0)

    y_row = iota((8, HEAD_DIM), 0)
    for n in range(G - 1):
        picked = jnp.where(slot_id == ahead[n][0], result, 0.0)
        message = jnp.zeros((8, HEAD_DIM), F32)
        for s in range(STEPS):
            line = jnp.sum(picked[s * ROWS : (s + 1) * ROWS], axis=0, keepdims=True)
            message = jnp.where(y_row == s, line, message)
        y_send[n] = message
    y_copies = [
        pltpu.make_async_remote_copy(
            src_ref=y_send.at[n], dst_ref=y_recv.at[n], send_sem=ys_sem.at[n], recv_sem=yr_sem.at[n],
            device_id={"group": lax.rem(my_g + n + 1, G)}, device_id_type=MESH,
        )
        for n in range(G - 1)
    ]
    for copy in y_copies:
        copy.start()

    for copy in z_copies:
        copy.wait_send()
    some = q_all.at[pl.ds(0, C - 1)]
    pltpu.make_async_copy(some, some, qs_sem).wait()
    some = a_send.at[pl.ds(0, C - 1)]
    pltpu.make_async_copy(some, some, as_sem).wait()
    some = o_send.at[pl.ds(0, C - 1)]
    pltpu.make_async_copy(some, some, os_sem).wait()

    @pl.when(kv_head == my_x)
    def _():
        if JJ > 1:
            some = kv_recv.at[pl.ds(0, JJ - 1)]
            pltpu.make_async_copy(some, some, ks_sem).wait()

    @pl.when(kv_head != my_x)
    def _():
        some = kv_recv.at[pl.ds(0, JJ)]
        pltpu.make_async_copy(some, some, ks_sem).wait()

    for n, copy in enumerate(y_copies):
        copy.wait_recv()
        came = y_recv[n]
        for s in range(STEPS):
            result = jnp.where((slot_id == behind[n][1]) & (row_id // ROWS == s), came[s : s + 1], result)
    for copy in y_copies:
        copy.wait_send()
    out_ref[0] = result[:ROWS].astype(BF16)
    out_ref[1] = result[ROWS:].astype(BF16)


def per_device(G, C, hidden, cache, lengths, source, target, wq, wkv, qgain, kgain, wo):
    D = hidden.shape[-1]
    BLK = cache.shape[1]
    JJ = C // KV_HEADS
    pieces = C // 8
    half = np.arange(HEAD_DIM // 2, dtype=np.float64)
    freq = (THETA ** (-2.0 * half / HEAD_DIM)).astype(np.float32)
    freq = jnp.asarray(np.concatenate([freq, freq])[None])
    vmem = lambda x: pltpu.VMEM(x.shape, x.dtype)
    smem = lambda x: pltpu.SMEM(x.shape, x.dtype)
    dma = pltpu.SemaphoreType.DMA
    operands = (hidden, cache, lengths, source, target, wq, wkv, qgain, kgain, wo, freq)
    return pl.pallas_call(
        functools.partial(kernel, G, C, D, BLK),
        out_shape=jax.ShapeDtypeStruct((STEPS, ROWS, D // C), BF16),
        in_specs=[pl.BlockSpec(memory_space=pltpu.HBM)] * len(operands),
        out_specs=pl.BlockSpec(memory_space=pltpu.VMEM),
        scratch_shapes=[
            vmem(hidden), vmem(cache), vmem(wq), vmem(wkv), vmem(wo), vmem(qgain), vmem(kgain), vmem(freq),
            smem(lengths), smem(source), smem(target),
            pltpu.VMEM((G - 1, SR, HEAD_DIM), BF16),
            pltpu.VMEM((G - 1, SR, HEAD_DIM), BF16),
            pltpu.VMEM((C, RQ, HEAD_DIM), BF16),
            pltpu.VMEM((SR, HEAD_DIM), BF16),
            pltpu.VMEM((max(2 * pieces, JJ), SR, HEAD_DIM), BF16),
            pltpu.VMEM((RQ, HEAD_DIM), F32),
            pltpu.VMEM((C, RQ + 16, HEAD_DIM), BF16),
            pltpu.VMEM((C, RQ + 16, HEAD_DIM), BF16),
            pltpu.VMEM((RQ, HEAD_DIM), F32),
            pltpu.VMEM((C, SR, D // C), BF16),
            pltpu.VMEM((C, SR, D // C), BF16),
            pltpu.VMEM((G - 1, 8, HEAD_DIM), F32),
            pltpu.VMEM((G - 1, 8, HEAD_DIM), F32),
            dma((10,)), dma((ROWS,)), dma((G - 1,)), dma((G - 1,)), dma, dma((KV_HEADS,)), dma, dma((2 * pieces,)),
            dma, dma, dma, dma, dma((G - 1,)), dma((G - 1,)),
        ],
        compiler_params=pltpu.CompilerParams(
            collective_id=0, has_side_effects=True, vmem_limit_bytes=48 * 1024 * 1024
        ),
    )(*operands)


def solution(mesh):
    in_specs = (
        P(None, "group", None),
        P("group", "ctx", None),
        P(),
        P(),
        P(),
        P(None, "ctx"),
        P(None, "ctx"),
        P(),
        P(),
        P("ctx", None),
    )
    return jax.shard_map(
        functools.partial(per_device, mesh.shape["group"], mesh.shape["ctx"]),
        mesh=mesh, in_specs=in_specs, out_specs=P(None, "group", "ctx"), check_vma=False,
    )
```

time: 350 us -> 51.9 us (0.15); the launches traced: 344 us -> 51.6 us
  blocking collectives: 102 us -> 0 us
  waiting for transfers between devices: 87.4 us -> 0 us
  local copies, waits for them, and re-layouts: 71.6 us -> 10 us
  other arithmetic: 52.4 us -> 0 us
  Pallas kernels: 0 us -> 41.6 us
  between operations: 13.8 us -> 0.03 us
  matrix products: 10.4 us -> 0 us
  starting transfers between devices: 6.03 us -> 0 us
    all_gather x4 -> x0, blocking collectives: 102 us -> none  [the longest x2 49.4 us: merged_2(): gathered = jax.tree.map(lambda a: lax.all_gather(a, axis), part)]
    reduce_scatter x1 -> x0, waiting for transfers between devices: 68.2 us -> none  [attend(): lax.psum_scatter(partial_out, 'ctx', scatter_dimension=2, tiled=True)]
    add x65 -> x0, other arithmetic: 46.6 us -> none  [the longest x31 44.8 us: combine_parts(): earlier[2] * early_scale[..., None] + later[2] * late_scale[..., None]]
    pallas_call x0 -> x1, Pallas kernels: none -> 41.6 us  [per_device(): pl.pallas_call(functools.partial(kernel, G, C, D, BLK), out_shape=jax.Sha...]
    dynamic_slice x34 -> x0, local copies, waits for them, and re-layouts: 25.4 us -> none  [take(): lax.dynamic_index_in_dim(a, source, 0, False)]
    all_to_all x1 -> x0, waiting for transfers between devices: 19.2 us -> none  [per_device(): lax.all_to_all(outgoing, 'group', split_axis=0, concat_axis=0, tiled=True)]
    slice x4 -> x0, local copies, waits for them, and re-layouts: 18.6 us -> none  [the longest x2 12.2 us: attend(): row_cache[:, :, KV_HEADS * HEAD_DIM:]]
    dot_general x7 -> x0, matrix products: 10.4 us -> none  [the longest x1 3.28 us: attend(): jnp.einsum('srgjd,rpgd->srgjp', grouped, cache_keys, preferred_element_ty...]
  transfers between devices with their start and end apart: 3 -> 0, of which waited for: 2 -> 0; matrix products, arithmetic and copies ran while one was open for 2% -> 0% of each run, Pallas kernels for 0% -> 0%
where the time goes in v1:
time: 51.9 us; the launch traced here: 51.6 us
  Pallas kernels  41.6 us (80%)
  local copies, waits for them, and re-layouts  10 us (19%)
    pallas_call x1, Pallas kernels, per_device(): pl.pallas_call(functools.partial(kernel, G, C, D, BLK), out_shape=jax.Sha...  41.6 us
    unnamed x20, local copies, waits for them, and re-layouts  10 us

profile of v1, /device:TPU:1, one launch (start us, length us, event | category | flops | bytes accessed | tf_op | source)
XLA Modules:
  0.0 51.6 jit_solution(4154590340997622244)
XLA Ops:
  0.0 1.4 %copy.12.wkv_h = bf16[4096,32]{1,0:T(8,128)(2,1)S(1)} copy(bf16[4096,32]{0,1:T(8,128)(2,1)} %param.17) | data formatting | bytes 524288 | tf_op args[6]
  1.4 0.0 copy-start
  1.4 1.6 %copy-done = bf16[4096,256]{1,0:T(8,128)(2,1)S(1)} copy-done((bf16[4096,256]{1,0:T(8,128)(2,1)S(1)}, bf16[4096,256]{1,0:T(8,128)(2,1)}, u32[]{:S(2)}) %copy-start) | copy-done | bytes 2097176
  3.0 0.0 copy-start.1
  3.0 1.6 %copy-done.1 = bf16[256,4096]{1,0:T(8,128)(2,1)S(1)} copy-done((bf16[256,4096]{1,0:T(8,128)(2,1)S(1)}, bf16[256,4096]{1,0:T(8,128)(2,1)}, u32[]{:S(2)}) %copy-start.1) | copy-done | bytes 2097176
  4.6 0.0 copy-start.2
  4.6 0.9 %copy-done.2 = bf16[2,8,4096]{2,1,0:T(8,128)(2,1)S(1)} copy-done((bf16[2,8,4096]{2,1,0:T(8,128)(2,1)S(1)}, bf16[2,8,4096]{2,1,0:T(8,128)(2,1)}, u32[]{:S(2)}) %copy-start.2) | copy-done | bytes 131096
  5.5 0.0 copy-start.3
  5.5 0.7 %copy-done.3 = s32[32]{0:T(128)S(1)} copy-done((s32[32]{0:T(128)S(1)}, s32[32]{0:T(128)}, u32[]{:S(2)}) %copy-start.3) | copy-done | bytes 152
  6.2 0.0 copy-start.4
  6.2 0.7 %copy-done.4 = s32[12]{0:T(128)S(1)} copy-done((s32[12]{0:T(128)S(1)}, s32[12]{0:T(128)}, u32[]{:S(2)}) %copy-start.4) | copy-done | bytes 72
  6.8 0.0 copy-start.5
  6.8 0.7 %copy-done.5 = s32[12]{0:T(128)S(1)} copy-done((s32[12]{0:T(128)S(1)}, s32[12]{0:T(128)}, u32[]{:S(2)}) %copy-start.5) | copy-done | bytes 72
  7.5 0.0 copy-start.6
  7.5 0.7 %copy-done.6 = bf16[128]{0:T(256)(128)(2,1)S(1)} copy-done((bf16[128]{0:T(256)(128)(2,1)S(1)}, bf16[128]{0:T(256)(128)(2,1)}, u32[]{:S(2)}) %copy-start.6) | copy-done | bytes 280
  8.1 0.0 copy-start.7
  8.1 0.7 %copy-done.7 = bf16[128]{0:T(256)(128)(2,1)S(1)} copy-done((bf16[128]{0:T(256)(128)(2,1)S(1)}, bf16[128]{0:T(256)(128)(2,1)}, u32[]{:S(2)}) %copy-start.7) | copy-done | bytes 280
  8.8 0.0 copy-start.8
  8.8 0.7 %copy-done.8 = f32[1,128]{1,0:T(1,128)S(1)} copy-done((f32[1,128]{1,0:T(1,128)S(1)}, f32[1,128]{1,0:T(1,128)}, u32[]{:S(2)}) %copy-start.8) | copy-done | bytes 536
  9.5 41.6 %shard_map.109 = bf16[2,8,128]{2,1,0:T(8,128)(2,1)S(1)} custom-call(bf16[2,8,4096]{2,1,0:T(8,128)(2,1)S(1)} %copy-done.2, bf16[8,512,1024]{2,1,0:T(8,128)(2,1)} %cache_h.1, s32[32]{0:T(128)S(1)} %copy-done.3, s32[12]{0:T(128)S(1)} %copy-done.4, s32[12]{0:T(128)S(1)} %copy-done.5, bf16[4096,256]{1,0:T(8,128)(2,1)S(1)} %copy-done, ...), custom_call_target="tpu_custom_call" | custom-call | tf_op jit(solution)/shard_map/pallas_call | solution.py:410
  51.0 0.6 %copy.14 = bf16[2,8,128]{2,1,0:T(8,128)(2,1)} copy(bf16[2,8,128]{2,1,0:T(8,128)(2,1)S(1)} %shard_map.109) | data formatting | bytes 8192
Async XLA Ops:
  1.4 1.6 %copy-start = (bf16[4096,256]{1,0:T(8,128)(2,1)S(1)}, bf16[4096,256]{1,0:T(8,128)(2,1)}, u32[]{:S(2)}) copy-start(bf16[4096,256]{1,0:T(8,128)(2,1)} %wq_h.1) | copy-start | bytes 6291460
  3.0 1.6 %copy-start.1 = (bf16[256,4096]{1,0:T(8,128)(2,1)S(1)}, bf16[256,4096]{1,0:T(8,128)(2,1)}, u32[]{:S(2)}) copy-start(bf16[256,4096]{1,0:T(8,128)(2,1)} %wo_h.1) | copy-start | bytes 6291460
  4.6 0.9 %copy-start.2 = (bf16[2,8,4096]{2,1,0:T(8,128)(2,1)S(1)}, bf16[2,8,4096]{2,1,0:T(8,128)(2,1)}, u32[]{:S(2)}) copy-start(bf16[2,8,4096]{2,1,0:T(8,128)(2,1)} %hidden_h.1) | copy-start | bytes 393220
  5.5 0.7 %copy-start.3 = (s32[32]{0:T(128)S(1)}, s32[32]{0:T(128)}, u32[]{:S(2)}) copy-start(s32[32]{0:T(128)} %lengths_h.1) | copy-start | bytes 388
  6.2 0.7 %copy-start.4 = (s32[12]{0:T(128)S(1)}, s32[12]{0:T(128)}, u32[]{:S(2)}) copy-start(s32[12]{0:T(128)} %source_h.1) | copy-start | bytes 148
  6.8 0.7 %copy-start.5 = (s32[12]{0:T(128)S(1)}, s32[12]{0:T(128)}, u32[]{:S(2)}) copy-start(s32[12]{0:T(128)} %target_h.1) | copy-start | bytes 148
  7.5 0.7 %copy-start.6 = (bf16[128]{0:T(256)(128)(2,1)S(1)}, bf16[128]{0:T(256)(128)(2,1)}, u32[]{:S(2)}) copy-start(bf16[128]{0:T(256)(128)(2,1)} %qgain_h.1) | copy-start | bytes 772
  8.1 0.7 %copy-start.7 = (bf16[128]{0:T(256)(128)(2,1)S(1)}, bf16[128]{0:T(256)(128)(2,1)}, u32[]{:S(2)}) copy-start(bf16[128]{0:T(256)(128)(2,1)} %kgain_h.1) | copy-start | bytes 772
  8.8 0.7 %copy-start.8 = (f32[1,128]{1,0:T(1,128)S(1)}, f32[1,128]{1,0:T(1,128)}, u32[]{:S(2)}) copy-start(f32[1,128]{1,0:T(1,128)} %constant.2.clone.freq_h) | copy-start | bytes 1540

commit v2 on v1

v2 whole, which is shorter than its diff:
```python
import functools
import math

import jax
import jax.numpy as jnp
import numpy as np
from jax import lax
from jax.experimental import pallas as pl
from jax.experimental.pallas import tpu as pltpu
from jax.sharding import PartitionSpec as P

MESH = pl.DeviceIdType.MESH
F32 = jnp.float32
BF16 = jnp.bfloat16

ROWS = 8
STEPS = 2
KV_HEADS = 4
HEAD_DIM = 128
LOCAL_HEADS = 2
Q = LOCAL_HEADS * STEPS
RQ = ROWS * Q
SR = STEPS * ROWS
HALF = RQ // 2
EPS = 1e-6
THETA = 1000000.0
FLOOR = -1e30
LOW = -1e29
PLANES = (1, 3, 2, 0)
FAR_FIRST = (2, 1, 3, 0)
QSCALE = HEAD_DIM**-0.5 * math.log2(math.e)


def iota(shape, dim):
    return lax.broadcasted_iota(jnp.int32, shape, dim)


def pick(order, n):
    return (sum(v << 2 * k for k, v in enumerate(order)) >> (2 * n)) & 3


def normed(x, gain):
    return x * lax.rsqrt(jnp.mean(x * x, axis=-1, keepdims=True) + EPS) * gain


def rotated(x, cos, sin):
    return x * cos + pltpu.roll(x, HEAD_DIM // 2, 1) * sin


def kernel(
    G, C, D, BLK,
    hidden_h, cache_h, lengths_h, source_h, target_h, wq_h, wkv_h, qgain_h, kgain_h, wo_h, freq_h,
    out_ref,
    hidden, cache, wq, wkv, wo, qgain, kgain, freq, lengths, source, target,
    raw, z_send, z_recv, pre, q_all, kv_pre, kv_send, kv_recv, a_send, a_recv, ml_send, ml_recv, mix,
    o_send, o_recv, y_send, y_recv,
    load_sem, cache_sem, zs_sem, zr_sem, qs_sem, qr_sem, ks_sem, kr_sem, as_sem, ar_sem, ms_sem, mr_sem,
    os_sem, or_sem, ys_sem, yr_sem,
):
    JJ = C // KV_HEADS
    J_BITS = JJ.bit_length() - 1
    KVW = 2 * KV_HEADS * HEAD_DIM // C
    PIECES = HEAD_DIM // KVW
    STAY = ROWS - (G - 1)
    my_g = lax.axis_index("group")
    my_c = lax.axis_index("ctx")
    my_x = my_c >> J_BITS
    my_low = my_c & (JJ - 1)
    drains = []

    def neighbour(plane, n):
        y = ((my_low >> 1) + pick(FAR_FIRST, n >> 1)) & (JJ // 2 - 1)
        return plane * JJ + y * 2 + ((my_low & 1) ^ (1 - (n & 1)))

    def remote(src, dst, send_sem, recv_sem, **dest):
        return pltpu.make_async_remote_copy(
            src_ref=src, dst_ref=dst, send_sem=send_sem, recv_sem=recv_sem, device_id=dest, device_id_type=MESH
        )

    def bytes_of(ref, sem):
        pltpu.make_async_copy(ref, ref, sem).wait()

    loads = [
        (hidden_h, hidden), (wkv_h, wkv), (wq_h, wq), (lengths_h, lengths), (source_h, source), (target_h, target),
        (freq_h, freq), (qgain_h, qgain), (kgain_h, kgain), (wo_h, wo),
    ]
    loads = [pltpu.make_async_copy(a, b, load_sem.at[n]) for n, (a, b) in enumerate(loads)]
    for load in loads[:-1]:
        load.start()
    cache_loads = [pltpu.make_async_copy(cache_h.at[r], cache.at[r], cache_sem.at[r]) for r in range(ROWS)]

    barrier = pltpu.get_barrier_semaphore()

    def greet(n, carry):
        pl.semaphore_signal(barrier, inc=1, device_id={"ctx": (my_c + n) & (C - 1)}, device_id_type=MESH)
        return carry

    for n in range(1, G):
        pl.semaphore_signal(barrier, inc=1, device_id={"group": (my_g + n) & (G - 1)}, device_id_type=MESH)
    lax.fori_loop(1, C, greet, 0)

    for load in loads[3:9]:
        load.wait()
    order = [jnp.int32(0)] * ROWS
    home = [jnp.int32(0)] * G
    listed = [False] * ROWS
    for e in range(source.shape[0]):
        s, t = source[e], target[e]
        off = ((t >> 3) - (s >> 3)) & (G - 1)
        out, back = (s >> 3) == my_g, (t >> 3) == my_g
        for n in range(1, G):
            order[STAY + n - 1] = order[STAY + n - 1] + jnp.where(out & (off == n), s & (ROWS - 1), 0)
            home[n] = home[n] + jnp.where(back & (off == G - n), t & (ROWS - 1), 0)
        for r in range(ROWS):
            listed[r] = listed[r] | (s == my_g * ROWS + r)
    count = jnp.int32(0)
    for r in range(ROWS):
        for n in range(min(r + 1, STAY)):
            order[n] = order[n] + jnp.where((count == n) & jnp.logical_not(listed[r]), r, 0)
        count = count + jnp.where(listed[r], 0, 1)
    row_lengths = [lengths[my_g * ROWS + order[r]] for r in range(ROWS)]

    table = (RQ + SR, HEAD_DIM)
    at, lane = iota(table, 0), iota(table, 1)
    row = jnp.where(at < RQ, at >> 2, (at - RQ) >> 1)
    position = at & 1
    for r in range(ROWS):
        position = position + jnp.where(row == r, row_lengths[r], 0)
    angle = position.astype(F32) * freq[...]
    cos = jnp.cos(angle)
    sin = jnp.sin(angle)
    sin = jnp.where(lane < HEAD_DIM // 2, -sin, sin)
    q_gain = qgain[...].astype(F32).reshape(1, HEAD_DIM) * QSCALE
    k_gain = kgain[...].astype(F32).reshape(1, HEAD_DIM)

    for load in loads[:3]:
        load.wait()
    for load in cache_loads:
        load.start()
    loads[-1].start()
    h = jnp.concatenate([hidden[0], hidden[1]], axis=0)
    q = jnp.dot(h, wq[...], preferred_element_type=F32).astype(BF16).astype(F32)
    kv = lax.dot_general(h, wkv[...], (((1,), (1,)), ((), ())), preferred_element_type=F32)
    kv = jnp.concatenate([kv.astype(BF16).astype(F32)] * PIECES, axis=1)
    parts = [q[:, j * HEAD_DIM : (j + 1) * HEAD_DIM] for j in range(LOCAL_HEADS)] + [kv]
    for n, x in enumerate(parts):
        for s in range(STEPS):
            raw[:, n * STEPS + s, :] = x[s * ROWS : (s + 1) * ROWS]
    raw[:, Q + STEPS :, :] = jnp.zeros((ROWS, 8 - Q - STEPS, HEAD_DIM), F32)
    for n in range(G - 1):
        z_send[n] = raw[home[n + 1]]

    def queries_of(half):
        rows = slice(half * HALF, (half + 1) * HALF)
        turned = rotated(normed(pre[rows, :], q_gain), cos[rows], sin[rows]).astype(BF16)
        q_all[half, my_c] = turned
        return turned

    for r in range(STAY):
        pre[r * Q : (r + 1) * Q, :] = raw[order[r], :Q, :]
        kv_pre[r * STEPS : (r + 1) * STEPS, :] = raw[order[r], Q : Q + STEPS, :]
    q_early = queries_of(0)
    pl.semaphore_wait(barrier, C - 1 + G - 1)

    z_copies = [
        remote(z_send.at[n], z_recv.at[n], zs_sem.at[n], zr_sem.at[n], group=(my_g + n + 1) & (G - 1))
        for n in range(G - 1)
    ]
    for copy in z_copies:
        copy.start()
    drains.append(lambda: [copy.wait_send() for copy in z_copies])

    def send_queries(half):
        def send_q(n, carry):
            plane = (my_x - pick(PLANES, n >> J_BITS)) & 3
            remote(
                q_all.at[half, my_c], q_all.at[half, my_c], qs_sem.at[half], qr_sem.at[half, my_x],
                ctx=neighbour(plane, n & (JJ - 1)),
            ).start()
            return carry

        lax.fori_loop(0, C - 1, send_q, 0)
        drains.append(lambda: bytes_of(q_all.at[half, pl.ds(0, C - 1)], qs_sem.at[half]))

    send_queries(0)

    ALL = JJ * HALF
    pi, pj = iota((ALL, ALL), 0), iota((ALL, ALL), 1)
    to_rows = pj == ((pi >> 2) & (JJ - 1)) * HALF + (pi >> (2 + J_BITS)) * Q + (pi & 3)
    to_devices = pj == ((pi >> 2) & 3) * (JJ * Q) + (pi >> 4) * Q + (pi & 3)
    to_rows = to_rows.astype(F32).astype(BF16)
    to_devices = to_devices.astype(F32).astype(BF16)
    gather = iota((JJ, 2 * ALL), 0) == ((iota((JJ, 2 * ALL), 1) >> 2) & (JJ - 1))
    gather = gather.astype(F32).astype(BF16)

    for copy in z_copies:
        copy.wait_recv()
    for n in range(1, G):
        r = STAY + n - 1
        pre[r * Q : (r + 1) * Q, :] = z_recv[G - 1 - n, :Q, :]
        kv_pre[r * STEPS : (r + 1) * STEPS, :] = z_recv[G - 1 - n, Q : Q + STEPS, :]
    q_late = queries_of(1)
    send_queries(1)

    kv_send[...] = kv_pre[...].astype(BF16)
    kv_bits = PIECES.bit_length() - 1
    kv_head = (my_c & (C // 2 - 1)) >> kv_bits
    kv_slot = ((my_c >> (C.bit_length() - 2)) << kv_bits) + (my_c & (PIECES - 1))

    def send_kv(n, carry):
        dest = kv_head * JJ + n

        @pl.when(dest != my_c)
        def _():
            remote(kv_send, kv_recv.at[kv_slot], ks_sem, kr_sem.at[kv_slot], ctx=dest).start()

        return carry

    lax.fori_loop(0, JJ, send_kv, 0)

    @pl.when(kv_head == my_x)
    def _():
        kv_recv[kv_slot] = kv_send[...]

    def drain_kv():
        @pl.when(kv_head == my_x)
        def _():
            if JJ > 1:
                bytes_of(kv_recv.at[pl.ds(0, JJ - 1)], ks_sem)

        @pl.when(kv_head != my_x)
        def _():
            bytes_of(kv_recv.at[pl.ds(0, JJ)], ks_sem)

    drains.append(drain_kv)

    place = iota((JJ * Q, BLK), 1) + my_c * BLK
    lanes = iota((JJ * Q, HEAD_DIM), 1) - (iota((JJ * Q, HEAD_DIM), 0) & 3)
    for load in cache_loads:
        load.wait()

    def attend(half):
        rows = range(half * ROWS // 2, (half + 1) * ROWS // 2)

        def one_plane(i, carry):
            g = (my_x + pick(PLANES, i)) & 3

            @pl.when(i == 3)
            def _():
                if JJ > 1:
                    bytes_of(q_all.at[half, pl.ds(0, JJ - 1)], qr_sem.at[half, g])

            @pl.when(i < 3)
            def _():
                bytes_of(q_all.at[half, pl.ds(0, JJ)], qr_sem.at[half, g])

            came = q_all[half, pl.ds(g * JJ, JJ)].reshape(ALL, HEAD_DIM)
            queries = jnp.dot(to_rows, came, preferred_element_type=F32).astype(BF16)
            k_at = pl.ds(pl.multiple_of(g * HEAD_DIM, HEAD_DIM), HEAD_DIM)
            v_at = pl.ds(pl.multiple_of((g + KV_HEADS) * HEAD_DIM, HEAD_DIM), HEAD_DIM)
            scores, peaks, weights, totals, sums, high, low = [], [], [], [], [], [], []
            for n, r in enumerate(rows):
                x = lax.dot_general(
                    queries[n * JJ * Q : (n + 1) * JJ * Q], cache[order[r], :, k_at], (((1,), (1,)), ((), ())),
                    preferred_element_type=F32,
                )
                scores.append(jnp.where(place < row_lengths[r], x, FLOOR))
            for x in scores:
                peaks.append(jnp.maximum(jnp.max(x, axis=1, keepdims=True), LOW).astype(BF16).astype(F32))
            for x, peak in zip(scores, peaks):
                x = jnp.exp2(x - peak)
                totals.append(jnp.sum(x, axis=1, keepdims=True))
                weights.append(x.astype(BF16))
            for x, r in zip(weights, rows):
                sums.append(jnp.dot(x, cache[order[r], :, v_at], preferred_element_type=F32).astype(BF16))
            for n, (peak, total) in enumerate(zip(peaks, totals)):
                rounded = total.astype(BF16).astype(F32)
                x = jnp.where(lanes == n * Q, peak, jnp.where(lanes == HALF + n * Q, rounded, 0.0))
                high.append(x.astype(BF16))
                low.append(jnp.where(lanes == HALF + n * Q, total - rounded, 0.0).astype(BF16))
            sums = jnp.dot(to_devices, jnp.concatenate(sums, axis=0), preferred_element_type=F32)
            stats = jnp.dot(gather, jnp.concatenate(high + low, axis=0), preferred_element_type=F32)
            a_send[half, pl.ds(g * JJ, JJ)] = sums.astype(BF16).reshape(JJ, HALF, HEAD_DIM)
            ml_send[half, pl.ds(g * JJ, JJ), 0, :] = stats

            def send_a(n, carry):
                dest = neighbour(g, n)
                remote(
                    a_send.at[half, dest], a_recv.at[half, my_c], as_sem.at[half], ar_sem.at[half], ctx=dest
                ).start()
                remote(
                    ml_send.at[half, dest], ml_recv.at[half, my_c], ms_sem.at[half], mr_sem.at[half], ctx=dest
                ).start()
                return carry

            lax.fori_loop(0, jnp.where(i == 3, JJ - 1, JJ), send_a, 0)
            return carry

        lax.fori_loop(0, KV_HEADS, one_plane, 0)
        drains.append(lambda: bytes_of(a_send.at[half, pl.ds(0, C - 1)], as_sem.at[half]))
        drains.append(lambda: bytes_of(ml_send.at[half, pl.ds(0, C - 1)], ms_sem.at[half]))
        a_recv[half, my_c] = a_send[half, my_c]
        ml_recv[half, my_c] = ml_send[half, my_c]

    attend(0)
    attend(1)

    def get_kv(n, carry):
        @pl.when((n >> kv_bits) * (C // 2) + my_x * PIECES + (n & (PIECES - 1)) != my_c)
        def _():
            bytes_of(kv_recv.at[n], kr_sem.at[n])

        return carry

    lax.fori_loop(0, 2 * PIECES, get_kv, 0)
    new = []
    piece = iota((SR, HEAD_DIM), 1) >> (KVW.bit_length() - 1)
    for kind in range(2):
        x = kv_recv[kind * PIECES].astype(F32)
        for n in range(1, PIECES):
            x = jnp.where(piece == n, kv_recv[kind * PIECES + n].astype(F32), x)
        new.append(x)
    new_key = rotated(normed(new[0], k_gain), cos[RQ:], sin[RQ:]).astype(BF16)
    new_value = new[1].astype(BF16)
    q_mine = jnp.concatenate([q_early, q_late], axis=0)
    scores = lax.dot_general(q_mine, new_key, (((1,), (1,)), ((), ())), preferred_element_type=F32)
    ti, tj = iota((RQ, SR), 0), iota((RQ, SR), 1)
    scores = jnp.where(((ti >> 2) == (tj >> 1)) & ((tj & 1) <= (ti & 1)), scores, FLOOR)
    new_peak = jnp.max(scores, axis=1, keepdims=True)
    weights = jnp.exp2(scores - new_peak)
    new_total = jnp.sum(weights, axis=1, keepdims=True)
    new_sums = jnp.dot(weights.astype(BF16), new_value, preferred_element_type=F32)

    for half in range(2):
        bytes_of(ml_recv.at[half, pl.ds(0, C - 1)], mr_sem.at[half])
        rows = slice(half * HALF, (half + 1) * HALF)
        stats = jnp.transpose(ml_recv[half, :, 0, :])
        peaks, totals = stats[:HALF], stats[HALF : 2 * HALF]
        highest = jnp.maximum(jnp.max(peaks, axis=1, keepdims=True), new_peak[rows])
        scale = jnp.exp2(peaks - highest)
        new_scale = jnp.exp2(new_peak[rows] - highest)
        norm = jnp.sum(scale * totals, axis=1, keepdims=True) + new_scale * new_total[rows]
        bytes_of(a_recv.at[half, pl.ds(0, C - 1)], ar_sem.at[half])
        acc = new_sums[rows] * new_scale
        for n in range(C):
            acc = acc + a_recv[half, n].astype(F32) * scale[:, n : n + 1]
        mix[rows, :] = acc / norm
    mixed = jnp.concatenate(
        [
            jnp.concatenate([mix[pl.ds(j * STEPS + s, ROWS, stride=Q), :] for s in range(STEPS)], axis=0)
            for j in range(LOCAL_HEADS)
        ],
        axis=1,
    ).astype(BF16)

    loads[-1].wait()
    quarter = D // KV_HEADS
    width = D // C

    def one_quarter(i, carry):
        g = (my_x + pick(FAR_FIRST, i)) & 3
        part = jnp.dot(
            mixed, wo[:, pl.ds(pl.multiple_of(g * quarter, quarter), quarter)], preferred_element_type=F32
        ).astype(BF16)
        for n in range(JJ):
            o_send[g * JJ + n] = part[:, n * width : (n + 1) * width]

        def send_o(n, carry):
            dest = neighbour(g, n)
            remote(o_send.at[dest], o_recv.at[my_c], os_sem, or_sem, ctx=dest).start()
            return carry

        lax.fori_loop(0, jnp.where(i == 3, JJ - 1, JJ), send_o, 0)
        return carry

    lax.fori_loop(0, KV_HEADS, one_quarter, 0)
    drains.append(lambda: bytes_of(o_send.at[pl.ds(0, C - 1)], os_sem))
    o_recv[my_c] = o_send[my_c]
    bytes_of(o_recv.at[pl.ds(0, C - 1)], or_sem)
    result = jnp.sum(o_recv[...].astype(F32), axis=0)

    for n in range(G - 1):
        for s in range(STEPS):
            y_send[n, s : s + 1, :] = result[s * ROWS + STAY + n : s * ROWS + STAY + n + 1]
        y_send[n, STEPS:, :] = jnp.zeros((8 - STEPS, HEAD_DIM), F32)
    y_copies = [
        remote(y_send.at[n], y_recv.at[n], ys_sem.at[n], yr_sem.at[n], group=(my_g + n + 1) & (G - 1))
        for n in range(G - 1)
    ]
    for copy in y_copies:
        copy.start()

    for drain in drains:
        drain()

    slot = iota((ROWS, HEAD_DIM), 0)
    lines = [jnp.zeros((ROWS, HEAD_DIM), F32)] * STEPS
    for s in range(STEPS):
        for r in range(STAY):
            lines[s] = jnp.where(slot == order[r], result[s * ROWS + r : s * ROWS + r + 1], lines[s])
    for n, copy in enumerate(y_copies):
        copy.wait_recv()
        for s in range(STEPS):
            lines[s] = jnp.where(slot == home[G - 1 - n], y_recv[n, s : s + 1, :], lines[s])
    for copy in y_copies:
        copy.wait_send()
    for s in range(STEPS):
        out_ref[s] = lines[s].astype(BF16)


def per_device(G, C, hidden, cache, lengths, source, target, wq, wkv, qgain, kgain, wo):
    D = hidden.shape[-1]
    BLK = cache.shape[1]
    JJ = C // KV_HEADS
    pieces = C // 8
    half = np.arange(HEAD_DIM // 2, dtype=np.float64)
    freq = (THETA ** (-2.0 * half / HEAD_DIM)).astype(np.float32)
    freq = jnp.asarray(np.concatenate([freq, freq])[None])
    vmem = lambda x: pltpu.VMEM(x.shape, x.dtype)
    smem = lambda x: pltpu.SMEM(x.shape, x.dtype)
    dma = pltpu.SemaphoreType.DMA
    wkv = wkv.T
    operands = (hidden, cache, lengths, source, target, wq, wkv, qgain, kgain, wo, freq)
    return pl.pallas_call(
        functools.partial(kernel, G, C, D, BLK),
        out_shape=jax.ShapeDtypeStruct((STEPS, ROWS, D // C), BF16),
        in_specs=[pl.BlockSpec(memory_space=pltpu.HBM)] * len(operands),
        out_specs=pl.BlockSpec(memory_space=pltpu.VMEM),
        scratch_shapes=[
            vmem(hidden), vmem(cache), vmem(wq), vmem(wkv), vmem(wo), vmem(qgain), vmem(kgain), vmem(freq),
            smem(lengths), smem(source), smem(target),
            pltpu.VMEM((ROWS, 8, HEAD_DIM), F32),
            pltpu.VMEM((G - 1, 8, HEAD_DIM), F32),
            pltpu.VMEM((G - 1, 8, HEAD_DIM), F32),
            pltpu.VMEM((RQ, HEAD_DIM), F32),
            pltpu.VMEM((2, C, HALF, HEAD_DIM), BF16),
            pltpu.VMEM((SR, HEAD_DIM), F32),
            pltpu.VMEM((SR, HEAD_DIM), BF16),
            pltpu.VMEM((max(2 * pieces, JJ), SR, HEAD_DIM), BF16),
            pltpu.VMEM((2, C, HALF, HEAD_DIM), BF16),
            pltpu.VMEM((2, C, HALF, HEAD_DIM), BF16),
            pltpu.VMEM((2, C, 1, HEAD_DIM), F32),
            pltpu.VMEM((2, C, 1, HEAD_DIM), F32),
            pltpu.VMEM((RQ, HEAD_DIM), F32),
            pltpu.VMEM((C, SR, D // C), BF16),
            pltpu.VMEM((C, SR, D // C), BF16),
            pltpu.VMEM((G - 1, 8, HEAD_DIM), F32),
            pltpu.VMEM((G - 1, 8, HEAD_DIM), F32),
            dma((10,)), dma((ROWS,)), dma((G - 1,)), dma((G - 1,)), dma((2,)), dma((2, KV_HEADS)), dma,
            dma((2 * pieces,)), dma((2,)), dma((2,)), dma((2,)), dma((2,)), dma, dma, dma((G - 1,)), dma((G - 1,)),
        ],
        compiler_params=pltpu.CompilerParams(
            collective_id=0, has_side_effects=True, vmem_limit_bytes=62 * 1024 * 1024
        ),
    )(*operands)


def solution(mesh):
    in_specs = (
        P(None, "group", None),
        P("group", "ctx", None),
        P(),
        P(),
        P(),
        P(None, "ctx"),
        P(None, "ctx"),
        P(),
        P(),
        P("ctx", None),
    )
    return jax.shard_map(
        functools.partial(per_device, mesh.shape["group"], mesh.shape["ctx"]),
        mesh=mesh, in_specs=in_specs, out_specs=P(None, "group", "ctx"), check_vma=False,
    )
```

time: 51.9 us -> 34.9 us (0.67)
  local copies, waits for them, and re-layouts: 10 us -> 1.28 us
  Pallas kernels: 41.6 us -> 33.5 us
    unnamed x20 -> x1, local copies, waits for them, and re-layouts: 10 us -> 1.28 us
    pallas_call x1, Pallas kernels: 41.6 us -> 33.5 us  [per_device(): pl.pallas_call(functools.partial(kernel, G, C, D, BLK), out_shape=jax.Sha...]
where the time goes in v2:
time: 34.9 us; the launch traced here: 34.7 us
  Pallas kernels  33.5 us (96%)
  local copies, waits for them, and re-layouts  1.28 us (4%)
    pallas_call x1, Pallas kernels, per_device(): pl.pallas_call(functools.partial(kernel, G, C, D, BLK), out_shape=jax.Sha...  33.5 us
    unnamed x1, local copies, waits for them, and re-layouts  1.28 us

profile of v2, /device:TPU:1, one launch (start us, length us, event | category | flops | bytes accessed | tf_op | source)
XLA Modules:
  0.0 34.7 jit_solution(15717334190467880874)
XLA Ops:
  0.0 33.5 %shard_map.109 = bf16[2,8,128]{2,1,0:T(8,128)(2,1)} custom-call(bf16[2,8,4096]{2,1,0:T(8,128)(2,1)} %hidden_h.1, bf16[8,512,1024]{2,1,0:T(8,128)(2,1)} %cache_h.1, s32[32]{0:T(128)} %lengths_h.1, s32[12]{0:T(128)} %source_h.1, s32[12]{0:T(128)} %target_h.1, bf16[4096,256]{1,0:T(8,128)(2,1)} %wq_h.1, bf16[32,4096]{1,0:T(8,128)(2,1)} %bitcast.1, ...), custom_call_target="tpu_custom_call" | custom-call | tf_op jit(solution)/shard_map/pallas_call | solution.py:424
  33.5 1.3 %copy.13 = bf16[2,8,128]{2,1,0:T(8,128)(2,1)} copy(bf16[2,8,128]{2,1,0:T(8,128)(2,1)} %shard_map.109) | data formatting | bytes 8192

commit v3 on v2

--- a/solution.py
+++ b/solution.py
@@ -21,13 +21,13 @@
 Q = LOCAL_HEADS * STEPS
 RQ = ROWS * Q
 SR = STEPS * ROWS
+CHUNKS = 4
 HALF = RQ // 2
 EPS = 1e-6
 THETA = 1000000.0
 FLOOR = -1e30
 LOW = -1e29
-PLANES = (1, 3, 2, 0)
-FAR_FIRST = (2, 1, 3, 0)
+FAR_FIRST = (2, 3, 1, 0)
 QSCALE = HEAD_DIM**-0.5 * math.log2(math.e)
 
 
@@ -36,6 +36,8 @@
 
 
 def pick(order, n):
+    if isinstance(n, int):
+        return order[n]
     return (sum(v << 2 * k for k, v in enumerate(order)) >> (2 * n)) & 3
 
 
@@ -52,7 +54,8 @@
     hidden_h, cache_h, lengths_h, source_h, target_h, wq_h, wkv_h, qgain_h, kgain_h, wo_h, freq_h,
     out_ref,
     hidden, cache, wq, wkv, wo, qgain, kgain, freq, lengths, source, target,
-    raw, z_send, z_recv, pre, q_all, kv_pre, kv_send, kv_recv, a_send, a_recv, ml_send, ml_recv, mix,
+    raw, z_send, z_recv, pre, q_early, q_late, kv_pre, kv_send, kv_recv, a_send_early, a_send_late,
+    a_recv_early, a_recv_late, ml_send, ml_recv, mix,
     o_send, o_recv, y_send, y_recv,
     load_sem, cache_sem, zs_sem, zr_sem, qs_sem, qr_sem, ks_sem, kr_sem, as_sem, ar_sem, ms_sem, mr_sem,
     os_sem, or_sem, ys_sem, yr_sem,
@@ -67,9 +70,12 @@
     my_x = my_c >> J_BITS
     my_low = my_c & (JJ - 1)
     drains = []
+    q_all = (q_early, q_late)
+    a_send, a_recv = (a_send_early, a_send_late), (a_recv_early, a_recv_late)
+    halves = (range(ROWS // 2), range(ROWS // 2, ROWS))
 
     def neighbour(plane, n):
-        y = ((my_low >> 1) + pick(FAR_FIRST, n >> 1)) & (JJ // 2 - 1)
+        y = ((my_low >> 1) ^ pick(FAR_FIRST, n >> 1)) & (JJ // 2 - 1)
         return plane * JJ + y * 2 + ((my_low & 1) ^ (1 - (n & 1)))
 
     def remote(src, dst, send_sem, recv_sem, **dest):
@@ -80,26 +86,28 @@
     def bytes_of(ref, sem):
         pltpu.make_async_copy(ref, ref, sem).wait()
 
-    loads = [
-        (hidden_h, hidden), (wkv_h, wkv), (wq_h, wq), (lengths_h, lengths), (source_h, source), (target_h, target),
-        (freq_h, freq), (qgain_h, qgain), (kgain_h, kgain), (wo_h, wo),
-    ]
-    loads = [pltpu.make_async_copy(a, b, load_sem.at[n]) for n, (a, b) in enumerate(loads)]
+    barrier = pltpu.get_barrier_semaphore()
+    for n in range(1, G):
+        pl.semaphore_signal(barrier, inc=1, device_id={"group": (my_g + n) & (G - 1)}, device_id_type=MESH)
+
+    def greet(n, carry):
+        dest = neighbour(my_x ^ pick(FAR_FIRST, n >> J_BITS), n & (JJ - 1))
+        pl.semaphore_signal(barrier, inc=1, device_id={"ctx": dest}, device_id_type=MESH)
+        return carry
+
+    lax.fori_loop(0, JJ, greet, 0)
+    depth = D // CHUNKS
+    copies = [(hidden_h, hidden), (wkv_h, wkv)]
+    copies += [(wq_h.at[pl.ds(n * depth, depth)], wq.at[pl.ds(n * depth, depth)]) for n in range(CHUNKS)]
+    copies += [(source_h, source), (target_h, target), (lengths_h, lengths), (freq_h, freq), (qgain_h, qgain)]
+    copies += [(kgain_h, kgain), (wo_h, wo)]
+    loads = [pltpu.make_async_copy(a, b, load_sem.at[n]) for n, (a, b) in enumerate(copies)]
     for load in loads[:-1]:
         load.start()
     cache_loads = [pltpu.make_async_copy(cache_h.at[r], cache.at[r], cache_sem.at[r]) for r in range(ROWS)]
-
-    barrier = pltpu.get_barrier_semaphore()
-
-    def greet(n, carry):
-        pl.semaphore_signal(barrier, inc=1, device_id={"ctx": (my_c + n) & (C - 1)}, device_id_type=MESH)
-        return carry
-
-    for n in range(1, G):
-        pl.semaphore_signal(barrier, inc=1, device_id={"group": (my_g + n) & (G - 1)}, device_id_type=MESH)
-    lax.fori_loop(1, C, greet, 0)
-
-    for load in loads[3:9]:
+    lax.fori_loop(JJ, C - 1, greet, 0)
+
+    for load in loads[2 + CHUNKS : -1]:
         load.wait()
     order = [jnp.int32(0)] * ROWS
     home = [jnp.int32(0)] * G
@@ -120,8 +128,7 @@
         count = count + jnp.where(listed[r], 0, 1)
     row_lengths = [lengths[my_g * ROWS + order[r]] for r in range(ROWS)]
 
-    table = (RQ + SR, HEAD_DIM)
-    at, lane = iota(table, 0), iota(table, 1)
+    at, lane = iota((RQ + SR, HEAD_DIM), 0), iota((RQ + SR, HEAD_DIM), 1)
     row = jnp.where(at < RQ, at >> 2, (at - RQ) >> 1)
     position = at & 1
     for r in range(ROWS):
@@ -133,15 +140,21 @@
     q_gain = qgain[...].astype(F32).reshape(1, HEAD_DIM) * QSCALE
     k_gain = kgain[...].astype(F32).reshape(1, HEAD_DIM)
 
-    for load in loads[:3]:
-        load.wait()
-    for load in cache_loads:
-        load.start()
-    loads[-1].start()
+    loads[0].wait()
     h = jnp.concatenate([hidden[0], hidden[1]], axis=0)
-    q = jnp.dot(h, wq[...], preferred_element_type=F32).astype(BF16).astype(F32)
+    loads[1].wait()
     kv = lax.dot_general(h, wkv[...], (((1,), (1,)), ((), ())), preferred_element_type=F32)
     kv = jnp.concatenate([kv.astype(BF16).astype(F32)] * PIECES, axis=1)
+    q = jnp.zeros((SR, wq.shape[1]), F32)
+    for n in range(CHUNKS):
+        loads[2 + n].wait()
+        if n == CHUNKS - 1:
+            for load in cache_loads:
+                load.start()
+            loads[-1].start()
+        at = slice(n * depth, (n + 1) * depth)
+        q = q + jnp.dot(h[:, at], wq[at, :], preferred_element_type=F32)
+    q = q.astype(BF16).astype(F32)
     parts = [q[:, j * HEAD_DIM : (j + 1) * HEAD_DIM] for j in range(LOCAL_HEADS)] + [kv]
     for n, x in enumerate(parts):
         for s in range(STEPS):
@@ -150,16 +163,6 @@
     for n in range(G - 1):
         z_send[n] = raw[home[n + 1]]
 
-    def queries_of(half):
-        rows = slice(half * HALF, (half + 1) * HALF)
-        turned = rotated(normed(pre[rows, :], q_gain), cos[rows], sin[rows]).astype(BF16)
-        q_all[half, my_c] = turned
-        return turned
-
-    for r in range(STAY):
-        pre[r * Q : (r + 1) * Q, :] = raw[order[r], :Q, :]
-        kv_pre[r * STEPS : (r + 1) * STEPS, :] = raw[order[r], Q : Q + STEPS, :]
-    q_early = queries_of(0)
     pl.semaphore_wait(barrier, C - 1 + G - 1)
 
     z_copies = [
@@ -171,23 +174,30 @@
     drains.append(lambda: [copy.wait_send() for copy in z_copies])
 
     def send_queries(half):
+        rows = slice(half * HALF, (half + 1) * HALF)
+        turned = rotated(normed(pre[rows, :], q_gain), cos[rows], sin[rows]).astype(BF16)
+        q_all[half][my_c] = turned
+
         def send_q(n, carry):
-            plane = (my_x - pick(PLANES, n >> J_BITS)) & 3
+            dest = neighbour(my_x ^ pick(FAR_FIRST, n >> J_BITS), n & (JJ - 1))
             remote(
-                q_all.at[half, my_c], q_all.at[half, my_c], qs_sem.at[half], qr_sem.at[half, my_x],
-                ctx=neighbour(plane, n & (JJ - 1)),
+                q_all[half].at[my_c], q_all[half].at[my_c], qs_sem.at[half], qr_sem.at[half, my_x], ctx=dest
             ).start()
             return carry
 
         lax.fori_loop(0, C - 1, send_q, 0)
-        drains.append(lambda: bytes_of(q_all.at[half, pl.ds(0, C - 1)], qs_sem.at[half]))
-
-    send_queries(0)
+        drains.append(lambda: bytes_of(q_all[half].at[pl.ds(0, C - 1)], qs_sem.at[half]))
+        return turned
+
+    for r in range(STAY):
+        pre[r * Q : (r + 1) * Q, :] = raw[order[r], :Q, :]
+        kv_pre[r * STEPS : (r + 1) * STEPS, :] = raw[order[r], Q : Q + STEPS, :]
+    queries = [send_queries(0)]
 
     ALL = JJ * HALF
-    pi, pj = iota((ALL, ALL), 0), iota((ALL, ALL), 1)
-    to_rows = pj == ((pi >> 2) & (JJ - 1)) * HALF + (pi >> (2 + J_BITS)) * Q + (pi & 3)
-    to_devices = pj == ((pi >> 2) & 3) * (JJ * Q) + (pi >> 4) * Q + (pi & 3)
+    at, to = iota((ALL, ALL), 0), iota((ALL, ALL), 1)
+    to_rows = to == ((at >> 2) & (JJ - 1)) * HALF + (at >> (2 + J_BITS)) * Q + (at & 3)
+    to_devices = to == ((at >> 2) & 3) * (JJ * Q) + (at >> 4) * Q + (at & 3)
     to_rows = to_rows.astype(F32).astype(BF16)
     to_devices = to_devices.astype(F32).astype(BF16)
     gather = iota((JJ, 2 * ALL), 0) == ((iota((JJ, 2 * ALL), 1) >> 2) & (JJ - 1))
@@ -199,8 +209,7 @@
         r = STAY + n - 1
         pre[r * Q : (r + 1) * Q, :] = z_recv[G - 1 - n, :Q, :]
         kv_pre[r * STEPS : (r + 1) * STEPS, :] = z_recv[G - 1 - n, Q : Q + STEPS, :]
-    q_late = queries_of(1)
-    send_queries(1)
+    queries.append(send_queries(1))
 
     kv_send[...] = kv_pre[...].astype(BF16)
     kv_bits = PIECES.bit_length() - 1
@@ -234,35 +243,37 @@
 
     drains.append(drain_kv)
 
-    place = iota((JJ * Q, BLK), 1) + my_c * BLK
-    lanes = iota((JJ * Q, HEAD_DIM), 1) - (iota((JJ * Q, HEAD_DIM), 0) & 3)
+    M = JJ * Q
+    place = iota((2 * M, BLK), 1) + my_c * BLK
+    lanes = iota((2 * M, HEAD_DIM), 1) - (iota((2 * M, HEAD_DIM), 0) & 3)
     for load in cache_loads:
         load.wait()
 
     def attend(half):
-        rows = range(half * ROWS // 2, (half + 1) * ROWS // 2)
-
-        def one_plane(i, carry):
-            g = (my_x + pick(PLANES, i)) & 3
-
-            @pl.when(i == 3)
-            def _():
-                if JJ > 1:
-                    bytes_of(q_all.at[half, pl.ds(0, JJ - 1)], qr_sem.at[half, g])
-
-            @pl.when(i < 3)
-            def _():
-                bytes_of(q_all.at[half, pl.ds(0, JJ)], qr_sem.at[half, g])
-
-            came = q_all[half, pl.ds(g * JJ, JJ)].reshape(ALL, HEAD_DIM)
-            queries = jnp.dot(to_rows, came, preferred_element_type=F32).astype(BF16)
-            k_at = pl.ds(pl.multiple_of(g * HEAD_DIM, HEAD_DIM), HEAD_DIM)
-            v_at = pl.ds(pl.multiple_of((g + KV_HEADS) * HEAD_DIM, HEAD_DIM), HEAD_DIM)
+        rows = halves[half]
+        send, recv = a_send[half], a_recv[half]
+
+        for x in FAR_FIRST:
+            if JJ > (x == 0):
+                bytes_of(q_all[half].at[pl.ds(0, JJ - (x == 0))], qr_sem.at[half, my_x ^ x])
+
+        def two_planes(i):
+            first = (my_x & 2) ^ (2 - 2 * i)
+            nearer = my_x ^ (3 - 2 * i)
+            last = my_x ^ (2 - 2 * i)
+            k_at = pl.ds(pl.multiple_of(first * HEAD_DIM, 2 * HEAD_DIM), 2 * HEAD_DIM)
+            v_at = pl.ds(pl.multiple_of((first + KV_HEADS) * HEAD_DIM, 2 * HEAD_DIM), 2 * HEAD_DIM)
+            came = [q_all[half][pl.ds((first + m) * JJ, JJ)].reshape(ALL, HEAD_DIM) for m in range(2)]
+            came = [jnp.dot(to_rows, x, preferred_element_type=F32).astype(BF16) for x in came]
+            blank = jnp.zeros((M, HEAD_DIM), BF16)
             scores, peaks, weights, totals, sums, high, low = [], [], [], [], [], [], []
             for n, r in enumerate(rows):
+                a, b = [x[n * M : (n + 1) * M] for x in came]
+                both = jnp.concatenate(
+                    [jnp.concatenate([a, blank], axis=1), jnp.concatenate([blank, b], axis=1)], axis=0
+                )
                 x = lax.dot_general(
-                    queries[n * JJ * Q : (n + 1) * JJ * Q], cache[order[r], :, k_at], (((1,), (1,)), ((), ())),
-                    preferred_element_type=F32,
+                    both, cache[order[r], :, k_at], (((1,), (1,)), ((), ())), preferred_element_type=F32
                 )
                 scores.append(jnp.where(place < row_lengths[r], x, FLOOR))
             for x in scores:
@@ -275,35 +286,40 @@
                 sums.append(jnp.dot(x, cache[order[r], :, v_at], preferred_element_type=F32).astype(BF16))
             for n, (peak, total) in enumerate(zip(peaks, totals)):
                 rounded = total.astype(BF16).astype(F32)
-                x = jnp.where(lanes == n * Q, peak, jnp.where(lanes == HALF + n * Q, rounded, 0.0))
+                n = rows[n] * Q
+                x = jnp.where(lanes == n, peak, jnp.where(lanes == RQ + n, rounded, 0.0))
                 high.append(x.astype(BF16))
-                low.append(jnp.where(lanes == HALF + n * Q, total - rounded, 0.0).astype(BF16))
-            sums = jnp.dot(to_devices, jnp.concatenate(sums, axis=0), preferred_element_type=F32)
-            stats = jnp.dot(gather, jnp.concatenate(high + low, axis=0), preferred_element_type=F32)
-            a_send[half, pl.ds(g * JJ, JJ)] = sums.astype(BF16).reshape(JJ, HALF, HEAD_DIM)
-            ml_send[half, pl.ds(g * JJ, JJ), 0, :] = stats
-
-            def send_a(n, carry):
-                dest = neighbour(g, n)
-                remote(
-                    a_send.at[half, dest], a_recv.at[half, my_c], as_sem.at[half], ar_sem.at[half], ctx=dest
-                ).start()
-                remote(
-                    ml_send.at[half, dest], ml_recv.at[half, my_c], ms_sem.at[half], mr_sem.at[half], ctx=dest
-                ).start()
+                low.append(jnp.where(lanes == RQ + n, total - rounded, 0.0).astype(BF16))
+            for m in range(2):
+                mine = slice(m * M, (m + 1) * M)
+                x = jnp.concatenate([x[mine, m * HEAD_DIM : (m + 1) * HEAD_DIM] for x in sums], axis=0)
+                x = jnp.dot(to_devices, x, preferred_element_type=F32)
+                send[pl.ds((first + m) * JJ, JJ)] = x.astype(BF16).reshape(JJ, HALF, HEAD_DIM)
+                x = jnp.concatenate([x[mine] for x in high + low], axis=0)
+                x = jnp.dot(gather, x, preferred_element_type=F32)
+                if half:
+                    x = x + ml_send[pl.ds((first + m) * JJ, JJ), 0, :]
+                ml_send[pl.ds((first + m) * JJ, JJ), 0, :] = x
+
+            def send_to(n, carry):
+                dest = neighbour(jnp.where((n >= JJ) == (i == 1), last, nearer), n & (JJ - 1))
+                remote(send.at[dest], recv.at[my_c], as_sem.at[half], ar_sem.at[half], ctx=dest).start()
+                if half:
+                    remote(ml_send.at[dest], ml_recv.at[my_c], ms_sem, mr_sem, ctx=dest).start()
+
                 return carry
 
-            lax.fori_loop(0, jnp.where(i == 3, JJ - 1, JJ), send_a, 0)
-            return carry
-
-        lax.fori_loop(0, KV_HEADS, one_plane, 0)
-        drains.append(lambda: bytes_of(a_send.at[half, pl.ds(0, C - 1)], as_sem.at[half]))
-        drains.append(lambda: bytes_of(ml_send.at[half, pl.ds(0, C - 1)], ms_sem.at[half]))
-        a_recv[half, my_c] = a_send[half, my_c]
-        ml_recv[half, my_c] = ml_send[half, my_c]
+            lax.fori_loop(0, 2 * JJ - i, send_to, 0)
+
+        two_planes(0)
+        two_planes(1)
+        drains.append(lambda: bytes_of(send.at[pl.ds(0, C - 1)], as_sem.at[half]))
+        recv[my_c] = send[my_c]
 
     attend(0)
     attend(1)
+    ml_recv[my_c] = ml_send[my_c]
+    drains.append(lambda: bytes_of(ml_send.at[pl.ds(0, C - 1)], ms_sem))
 
     def get_kv(n, carry):
         @pl.when((n >> kv_bits) * (C // 2) + my_x * PIECES + (n & (PIECES - 1)) != my_c)
@@ -322,29 +338,29 @@
         new.append(x)
     new_key = rotated(normed(new[0], k_gain), cos[RQ:], sin[RQ:]).astype(BF16)
     new_value = new[1].astype(BF16)
-    q_mine = jnp.concatenate([q_early, q_late], axis=0)
+    q_mine = jnp.concatenate(queries, axis=0)
     scores = lax.dot_general(q_mine, new_key, (((1,), (1,)), ((), ())), preferred_element_type=F32)
-    ti, tj = iota((RQ, SR), 0), iota((RQ, SR), 1)
+    ti, tj = iota(scores.shape, 0), iota(scores.shape, 1)
     scores = jnp.where(((ti >> 2) == (tj >> 1)) & ((tj & 1) <= (ti & 1)), scores, FLOOR)
     new_peak = jnp.max(scores, axis=1, keepdims=True)
     weights = jnp.exp2(scores - new_peak)
     new_total = jnp.sum(weights, axis=1, keepdims=True)
     new_sums = jnp.dot(weights.astype(BF16), new_value, preferred_element_type=F32)
 
+    bytes_of(ml_recv.at[pl.ds(0, C - 1)], mr_sem)
+    stats = jnp.transpose(ml_recv[:, 0, :])
+    peaks, totals = stats[:RQ], stats[RQ : 2 * RQ]
+    highest = jnp.maximum(jnp.max(peaks, axis=1, keepdims=True), new_peak)
+    scale = jnp.exp2(peaks - highest)
+    new_scale = jnp.exp2(new_peak - highest)
+    norm = jnp.sum(scale * totals, axis=1, keepdims=True) + new_scale * new_total
     for half in range(2):
-        bytes_of(ml_recv.at[half, pl.ds(0, C - 1)], mr_sem.at[half])
+        bytes_of(a_recv[half].at[pl.ds(0, C - 1)], ar_sem.at[half])
         rows = slice(half * HALF, (half + 1) * HALF)
-        stats = jnp.transpose(ml_recv[half, :, 0, :])
-        peaks, totals = stats[:HALF], stats[HALF : 2 * HALF]
-        highest = jnp.maximum(jnp.max(peaks, axis=1, keepdims=True), new_peak[rows])
-        scale = jnp.exp2(peaks - highest)
-        new_scale = jnp.exp2(new_peak[rows] - highest)
-        norm = jnp.sum(scale * totals, axis=1, keepdims=True) + new_scale * new_total[rows]
-        bytes_of(a_recv.at[half, pl.ds(0, C - 1)], ar_sem.at[half])
-        acc = new_sums[rows] * new_scale
+        acc = [(new_sums * new_scale)[rows]] + [jnp.zeros((HALF, HEAD_DIM), F32)] * 3
         for n in range(C):
-            acc = acc + a_recv[half, n].astype(F32) * scale[:, n : n + 1]
-        mix[rows, :] = acc / norm
+            acc[n & 3] = acc[n & 3] + a_recv[half][n].astype(F32) * scale[rows, n : n + 1]
+        mix[rows, :] = ((acc[0] + acc[1]) + (acc[2] + acc[3])) / norm[rows]
     mixed = jnp.concatenate(
         [
             jnp.concatenate([mix[pl.ds(j * STEPS + s, ROWS, stride=Q), :] for s in range(STEPS)], axis=0)
@@ -357,8 +373,8 @@
     quarter = D // KV_HEADS
     width = D // C
 
-    def one_quarter(i, carry):
-        g = (my_x + pick(FAR_FIRST, i)) & 3
+    for i in range(KV_HEADS):
+        g = my_x ^ FAR_FIRST[i]
         part = jnp.dot(
             mixed, wo[:, pl.ds(pl.multiple_of(g * quarter, quarter), quarter)], preferred_element_type=F32
         ).astype(BF16)
@@ -370,10 +386,7 @@
             remote(o_send.at[dest], o_recv.at[my_c], os_sem, or_sem, ctx=dest).start()
             return carry
 
-        lax.fori_loop(0, jnp.where(i == 3, JJ - 1, JJ), send_o, 0)
-        return carry
-
-    lax.fori_loop(0, KV_HEADS, one_quarter, 0)
+        lax.fori_loop(0, JJ - (FAR_FIRST[i] == 0), send_o, 0)
     drains.append(lambda: bytes_of(o_send.at[pl.ds(0, C - 1)], os_sem))
     o_recv[my_c] = o_send[my_c]
     bytes_of(o_recv.at[pl.ds(0, C - 1)], or_sem)
@@ -433,21 +446,24 @@
             pltpu.VMEM((G - 1, 8, HEAD_DIM), F32),
             pltpu.VMEM((G - 1, 8, HEAD_DIM), F32),
             pltpu.VMEM((RQ, HEAD_DIM), F32),
-            pltpu.VMEM((2, C, HALF, HEAD_DIM), BF16),
+            pltpu.VMEM((C, HALF, HEAD_DIM), BF16),
+            pltpu.VMEM((C, HALF, HEAD_DIM), BF16),
             pltpu.VMEM((SR, HEAD_DIM), F32),
             pltpu.VMEM((SR, HEAD_DIM), BF16),
             pltpu.VMEM((max(2 * pieces, JJ), SR, HEAD_DIM), BF16),
-            pltpu.VMEM((2, C, HALF, HEAD_DIM), BF16),
-            pltpu.VMEM((2, C, HALF, HEAD_DIM), BF16),
-            pltpu.VMEM((2, C, 1, HEAD_DIM), F32),
-            pltpu.VMEM((2, C, 1, HEAD_DIM), F32),
+            pltpu.VMEM((C, HALF, HEAD_DIM), BF16),
+            pltpu.VMEM((C, HALF, HEAD_DIM), BF16),
+            pltpu.VMEM((C, HALF, HEAD_DIM), BF16),
+            pltpu.VMEM((C, HALF, HEAD_DIM), BF16),
+            pltpu.VMEM((C, 1, HEAD_DIM), F32),
+            pltpu.VMEM((C, 1, HEAD_DIM), F32),
             pltpu.VMEM((RQ, HEAD_DIM), F32),
             pltpu.VMEM((C, SR, D // C), BF16),
             pltpu.VMEM((C, SR, D // C), BF16),
             pltpu.VMEM((G - 1, 8, HEAD_DIM), F32),
             pltpu.VMEM((G - 1, 8, HEAD_DIM), F32),
-            dma((10,)), dma((ROWS,)), dma((G - 1,)), dma((G - 1,)), dma((2,)), dma((2, KV_HEADS)), dma,
-            dma((2 * pieces,)), dma((2,)), dma((2,)), dma((2,)), dma((2,)), dma, dma, dma((G - 1,)), dma((G - 1,)),
+            dma((9 + CHUNKS,)), dma((ROWS,)), dma((G - 1,)), dma((G - 1,)), dma((2,)), dma((2, KV_HEADS)), dma,
+            dma((2 * pieces,)), dma((2,)), dma((2,)), dma, dma, dma, dma, dma((G - 1,)), dma((G - 1,)),
         ],
         compiler_params=pltpu.CompilerParams(
             collective_id=0, has_side_effects=True, vmem_limit_bytes=62 * 1024 * 1024

time: 34.9 us -> 33.7 us (0.966)
  Pallas kernels: 33.5 us -> 32.3 us
    pallas_call x1, Pallas kernels: 33.5 us -> 32.3 us  [per_device(): pl.pallas_call(functools.partial(kernel, G, C, D, BLK), out_shape=jax.Sha...]
where the time goes in v3:
time: 33.7 us; the launch traced here: 33.6 us
  Pallas kernels  32.3 us (96%)
  local copies, waits for them, and re-layouts  1.28 us (4%)
    pallas_call x1, Pallas kernels, per_device(): pl.pallas_call(functools.partial(kernel, G, C, D, BLK), out_shape=jax.Sha...  32.3 us
    unnamed x1, local copies, waits for them, and re-layouts  1.28 us

profile of v3, /device:TPU:1, one launch (start us, length us, event | category | flops | bytes accessed | tf_op | source)
XLA Modules:
  0.0 33.6 jit_solution(17417177423992135124)
XLA Ops:
  0.0 32.3 %shard_map.109 = bf16[2,8,128]{2,1,0:T(8,128)(2,1)} custom-call(bf16[2,8,4096]{2,1,0:T(8,128)(2,1)} %hidden_h.1, bf16[8,512,1024]{2,1,0:T(8,128)(2,1)} %cache_h.1, s32[32]{0:T(128)} %lengths_h.1, s32[12]{0:T(128)} %source_h.1, s32[12]{0:T(128)} %target_h.1, bf16[4096,256]{1,0:T(8,128)(2,1)} %wq_h.1, bf16[32,4096]{1,0:T(8,128)(2,1)} %bitcast.1, ...), custom_call_target="tpu_custom_call" | custom-call | tf_op jit(solution)/shard_map/pallas_call | solution.py:437
  32.3 1.3 %copy.13 = bf16[2,8,128]{2,1,0:T(8,128)(2,1)} copy(bf16[2,8,128]{2,1,0:T(8,128)(2,1)} %shard_map.109) | data formatting | bytes 8192

commit v4 on v3

--- a/solution.py
+++ b/solution.py
@@ -21,7 +21,6 @@
 Q = LOCAL_HEADS * STEPS
 RQ = ROWS * Q
 SR = STEPS * ROWS
-CHUNKS = 4
 HALF = RQ // 2
 EPS = 1e-6
 THETA = 1000000.0
@@ -54,10 +53,9 @@
     hidden_h, cache_h, lengths_h, source_h, target_h, wq_h, wkv_h, qgain_h, kgain_h, wo_h, freq_h,
     out_ref,
     hidden, cache, wq, wkv, wo, qgain, kgain, freq, lengths, source, target,
-    raw, z_send, z_recv, pre, q_early, q_late, kv_pre, kv_send, kv_recv, a_send_early, a_send_late,
-    a_recv_early, a_recv_late, ml_send, ml_recv, mix,
+    raw, z_send, z_recv, pre, q_early, q_late, kv_pre, kv_send, kv_recv, a_send, a_recv, ml_send, ml_recv, mix,
     o_send, o_recv, y_send, y_recv,
-    load_sem, cache_sem, zs_sem, zr_sem, qs_sem, qr_sem, ks_sem, kr_sem, as_sem, ar_sem, ms_sem, mr_sem,
+    load_sem, zs_sem, zr_sem, qs_sem, qr_sem, ks_sem, kr_sem, as_sem, ar_sem, ms_sem, mr_sem,
     os_sem, or_sem, ys_sem, yr_sem,
 ):
     JJ = C // KV_HEADS
@@ -71,7 +69,6 @@
     my_low = my_c & (JJ - 1)
     drains = []
     q_all = (q_early, q_late)
-    a_send, a_recv = (a_send_early, a_send_late), (a_recv_early, a_recv_late)
     halves = (range(ROWS // 2), range(ROWS // 2, ROWS))
 
     def neighbour(plane, n):
@@ -95,19 +92,15 @@
         pl.semaphore_signal(barrier, inc=1, device_id={"ctx": dest}, device_id_type=MESH)
         return carry
 
-    lax.fori_loop(0, JJ, greet, 0)
-    depth = D // CHUNKS
-    copies = [(hidden_h, hidden), (wkv_h, wkv)]
-    copies += [(wq_h.at[pl.ds(n * depth, depth)], wq.at[pl.ds(n * depth, depth)]) for n in range(CHUNKS)]
-    copies += [(source_h, source), (target_h, target), (lengths_h, lengths), (freq_h, freq), (qgain_h, qgain)]
-    copies += [(kgain_h, kgain), (wo_h, wo)]
+    copies = [(wq_h, wq), (hidden_h, hidden), (wkv_h, wkv), (source_h, source), (target_h, target)]
+    copies += [(lengths_h, lengths), (freq_h, freq), (qgain_h, qgain), (kgain_h, kgain)]
+    copies += [(cache_h, cache), (wo_h, wo)]
     loads = [pltpu.make_async_copy(a, b, load_sem.at[n]) for n, (a, b) in enumerate(copies)]
-    for load in loads[:-1]:
+    for load in loads[:-2]:
         load.start()
-    cache_loads = [pltpu.make_async_copy(cache_h.at[r], cache.at[r], cache_sem.at[r]) for r in range(ROWS)]
-    lax.fori_loop(JJ, C - 1, greet, 0)
-
-    for load in loads[2 + CHUNKS : -1]:
+    lax.fori_loop(0, C - 1, greet, 0)
+
+    for load in loads[3:-2]:
         load.wait()
     order = [jnp.int32(0)] * ROWS
     home = [jnp.int32(0)] * G
@@ -140,21 +133,15 @@
     q_gain = qgain[...].astype(F32).reshape(1, HEAD_DIM) * QSCALE
     k_gain = kgain[...].astype(F32).reshape(1, HEAD_DIM)
 
-    loads[0].wait()
+    loads[1].wait()
+    loads[2].wait()
     h = jnp.concatenate([hidden[0], hidden[1]], axis=0)
-    loads[1].wait()
     kv = lax.dot_general(h, wkv[...], (((1,), (1,)), ((), ())), preferred_element_type=F32)
     kv = jnp.concatenate([kv.astype(BF16).astype(F32)] * PIECES, axis=1)
-    q = jnp.zeros((SR, wq.shape[1]), F32)
-    for n in range(CHUNKS):
-        loads[2 + n].wait()
-        if n == CHUNKS - 1:
-            for load in cache_loads:
-                load.start()
-            loads[-1].start()
-        at = slice(n * depth, (n + 1) * depth)
-        q = q + jnp.dot(h[:, at], wq[at, :], preferred_element_type=F32)
-    q = q.astype(BF16).astype(F32)
+    loads[0].wait()
+    for load in loads[-2:]:
+        load.start()
+    q = jnp.dot(h, wq[...], preferred_element_type=F32).astype(BF16).astype(F32)
     parts = [q[:, j * HEAD_DIM : (j + 1) * HEAD_DIM] for j in range(LOCAL_HEADS)] + [kv]
     for n, x in enumerate(parts):
         for s in range(STEPS):
@@ -165,13 +152,9 @@
 
     pl.semaphore_wait(barrier, C - 1 + G - 1)
 
-    z_copies = [
-        remote(z_send.at[n], z_recv.at[n], zs_sem.at[n], zr_sem.at[n], group=(my_g + n + 1) & (G - 1))
-        for n in range(G - 1)
-    ]
-    for copy in z_copies:
-        copy.start()
-    drains.append(lambda: [copy.wait_send() for copy in z_copies])
+    for n in range(G - 1):
+        remote(z_send.at[n], z_recv.at[n], zs_sem, zr_sem, group=(my_g + n + 1) & (G - 1)).start()
+    drains.append(lambda: bytes_of(z_send, zs_sem))
 
     def send_queries(half):
         rows = slice(half * HALF, (half + 1) * HALF)
@@ -181,7 +164,7 @@
         def send_q(n, carry):
             dest = neighbour(my_x ^ pick(FAR_FIRST, n >> J_BITS), n & (JJ - 1))
             remote(
-                q_all[half].at[my_c], q_all[half].at[my_c], qs_sem.at[half], qr_sem.at[half, my_x], ctx=dest
+                q_all[half].at[my_c], q_all[half].at[my_c], qs_sem.at[half], qr_sem.at[half], ctx=dest
             ).start()
             return carry
 
@@ -203,8 +186,7 @@
     gather = iota((JJ, 2 * ALL), 0) == ((iota((JJ, 2 * ALL), 1) >> 2) & (JJ - 1))
     gather = gather.astype(F32).astype(BF16)
 
-    for copy in z_copies:
-        copy.wait_recv()
+    bytes_of(z_recv, zr_sem)
     for n in range(1, G):
         r = STAY + n - 1
         pre[r * Q : (r + 1) * Q, :] = z_recv[G - 1 - n, :Q, :]
@@ -221,7 +203,7 @@
 
         @pl.when(dest != my_c)
         def _():
-            remote(kv_send, kv_recv.at[kv_slot], ks_sem, kr_sem.at[kv_slot], ctx=dest).start()
+            remote(kv_send, kv_recv.at[kv_slot], ks_sem, kr_sem, ctx=dest).start()
 
         return carry
 
@@ -246,16 +228,13 @@
     M = JJ * Q
     place = iota((2 * M, BLK), 1) + my_c * BLK
     lanes = iota((2 * M, HEAD_DIM), 1) - (iota((2 * M, HEAD_DIM), 0) & 3)
-    for load in cache_loads:
-        load.wait()
+    loads[-2].wait()
 
     def attend(half):
         rows = halves[half]
-        send, recv = a_send[half], a_recv[half]
-
-        for x in FAR_FIRST:
-            if JJ > (x == 0):
-                bytes_of(q_all[half].at[pl.ds(0, JJ - (x == 0))], qr_sem.at[half, my_x ^ x])
+        send, recv = a_send.at[half], a_recv.at[half]
+
+        bytes_of(q_all[half].at[pl.ds(0, C - 1)], qr_sem.at[half])
 
         def two_planes(i):
             first = (my_x & 2) ^ (2 - 2 * i)
@@ -303,32 +282,36 @@
 
             def send_to(n, carry):
                 dest = neighbour(jnp.where((n >= JJ) == (i == 1), last, nearer), n & (JJ - 1))
-                remote(send.at[dest], recv.at[my_c], as_sem.at[half], ar_sem.at[half], ctx=dest).start()
+                remote(send.at[dest], recv.at[my_c], as_sem, ar_sem, ctx=dest).start()
                 if half:
                     remote(ml_send.at[dest], ml_recv.at[my_c], ms_sem, mr_sem, ctx=dest).start()
 
                 return carry
 
-            lax.fori_loop(0, 2 * JJ - i, send_to, 0)
+            if half:
+                for n in range(2 * JJ - i):
+                    send_to(n, 0)
+            else:
+                lax.fori_loop(0, 2 * JJ - i, send_to, 0)
 
         two_planes(0)
         two_planes(1)
-        drains.append(lambda: bytes_of(send.at[pl.ds(0, C - 1)], as_sem.at[half]))
         recv[my_c] = send[my_c]
 
     attend(0)
     attend(1)
     ml_recv[my_c] = ml_send[my_c]
+    drains.append(lambda: bytes_of(a_send.at[:, pl.ds(0, C - 1)], as_sem))
     drains.append(lambda: bytes_of(ml_send.at[pl.ds(0, C - 1)], ms_sem))
 
-    def get_kv(n, carry):
-        @pl.when((n >> kv_bits) * (C // 2) + my_x * PIECES + (n & (PIECES - 1)) != my_c)
-        def _():
-            bytes_of(kv_recv.at[n], kr_sem.at[n])
-
-        return carry
-
-    lax.fori_loop(0, 2 * PIECES, get_kv, 0)
+    @pl.when(kv_head == my_x)
+    def _():
+        bytes_of(kv_recv.at[pl.ds(0, 2 * PIECES - 1)], kr_sem)
+
+    @pl.when(kv_head != my_x)
+    def _():
+        bytes_of(kv_recv.at[pl.ds(0, 2 * PIECES)], kr_sem)
+
     new = []
     piece = iota((SR, HEAD_DIM), 1) >> (KVW.bit_length() - 1)
     for kind in range(2):
@@ -354,12 +337,12 @@
     scale = jnp.exp2(peaks - highest)
     new_scale = jnp.exp2(new_peak - highest)
     norm = jnp.sum(scale * totals, axis=1, keepdims=True) + new_scale * new_total
+    bytes_of(a_recv.at[:, pl.ds(0, C - 1)], ar_sem)
     for half in range(2):
-        bytes_of(a_recv[half].at[pl.ds(0, C - 1)], ar_sem.at[half])
         rows = slice(half * HALF, (half + 1) * HALF)
         acc = [(new_sums * new_scale)[rows]] + [jnp.zeros((HALF, HEAD_DIM), F32)] * 3
         for n in range(C):
-            acc[n & 3] = acc[n & 3] + a_recv[half][n].astype(F32) * scale[rows, n : n + 1]
+            acc[n & 3] = acc[n & 3] + a_recv[half, n].astype(F32) * scale[rows, n : n + 1]
         mix[rows, :] = ((acc[0] + acc[1]) + (acc[2] + acc[3])) / norm[rows]
     mixed = jnp.concatenate(
         [
@@ -380,13 +363,9 @@
         ).astype(BF16)
         for n in range(JJ):
             o_send[g * JJ + n] = part[:, n * width : (n + 1) * width]
-
-        def send_o(n, carry):
+        for n in range(JJ - (FAR_FIRST[i] == 0)):
             dest = neighbour(g, n)
             remote(o_send.at[dest], o_recv.at[my_c], os_sem, or_sem, ctx=dest).start()
-            return carry
-
-        lax.fori_loop(0, JJ - (FAR_FIRST[i] == 0), send_o, 0)
     drains.append(lambda: bytes_of(o_send.at[pl.ds(0, C - 1)], os_sem))
     o_recv[my_c] = o_send[my_c]
     bytes_of(o_recv.at[pl.ds(0, C - 1)], or_sem)
@@ -396,12 +375,8 @@
         for s in range(STEPS):
             y_send[n, s : s + 1, :] = result[s * ROWS + STAY + n : s * ROWS + STAY + n + 1]
         y_send[n, STEPS:, :] = jnp.zeros((8 - STEPS, HEAD_DIM), F32)
-    y_copies = [
-        remote(y_send.at[n], y_recv.at[n], ys_sem.at[n], yr_sem.at[n], group=(my_g + n + 1) & (G - 1))
-        for n in range(G - 1)
-    ]
-    for copy in y_copies:
-        copy.start()
+    for n in range(G - 1):
+        remote(y_send.at[n], y_recv.at[n], ys_sem, yr_sem, group=(my_g + n + 1) & (G - 1)).start()
 
     for drain in drains:
         drain()
@@ -411,12 +386,11 @@
     for s in range(STEPS):
         for r in range(STAY):
             lines[s] = jnp.where(slot == order[r], result[s * ROWS + r : s * ROWS + r + 1], lines[s])
-    for n, copy in enumerate(y_copies):
-        copy.wait_recv()
+    bytes_of(y_recv, yr_sem)
+    for n in range(G - 1):
         for s in range(STEPS):
             lines[s] = jnp.where(slot == home[G - 1 - n], y_recv[n, s : s + 1, :], lines[s])
-    for copy in y_copies:
-        copy.wait_send()
+    bytes_of(y_send, ys_sem)
     for s in range(STEPS):
         out_ref[s] = lines[s].astype(BF16)
 
@@ -451,10 +425,8 @@
             pltpu.VMEM((SR, HEAD_DIM), F32),
             pltpu.VMEM((SR, HEAD_DIM), BF16),
             pltpu.VMEM((max(2 * pieces, JJ), SR, HEAD_DIM), BF16),
-            pltpu.VMEM((C, HALF, HEAD_DIM), BF16),
-            pltpu.VMEM((C, HALF, HEAD_DIM), BF16),
-            pltpu.VMEM((C, HALF, HEAD_DIM), BF16),
-            pltpu.VMEM((C, HALF, HEAD_DIM), BF16),
+            pltpu.VMEM((2, C, HALF, HEAD_DIM), BF16),
+            pltpu.VMEM((2, C, HALF, HEAD_DIM), BF16),
             pltpu.VMEM((C, 1, HEAD_DIM), F32),
             pltpu.VMEM((C, 1, HEAD_DIM), F32),
             pltpu.VMEM((RQ, HEAD_DIM), F32),
@@ -462,8 +434,7 @@
             pltpu.VMEM((C, SR, D // C), BF16),
             pltpu.VMEM((G - 1, 8, HEAD_DIM), F32),
             pltpu.VMEM((G - 1, 8, HEAD_DIM), F32),
-            dma((9 + CHUNKS,)), dma((ROWS,)), dma((G - 1,)), dma((G - 1,)), dma((2,)), dma((2, KV_HEADS)), dma,
-            dma((2 * pieces,)), dma((2,)), dma((2,)), dma, dma, dma, dma, dma((G - 1,)), dma((G - 1,)),
+            dma((11,)), dma, dma, dma((2,)), dma((2,)), dma, dma, dma, dma, dma, dma, dma, dma, dma, dma,
         ],
         compiler_params=pltpu.CompilerParams(
             collective_id=0, has_side_effects=True, vmem_limit_bytes=62 * 1024 * 1024

time: 33.7 us -> 33.2 us (0.985)
  Pallas kernels: 32.3 us -> 31.8 us
    pallas_call x1, Pallas kernels: 32.3 us -> 31.8 us  [per_device(): pl.pallas_call(functools.partial(kernel, G, C, D, BLK), out_shape=jax.Sha...]
where the time goes in v4:
time: 33.2 us; the launch traced here: 33 us
  Pallas kernels  31.8 us (96%)
  local copies, waits for them, and re-layouts  1.28 us (4%)
    pallas_call x1, Pallas kernels, per_device(): pl.pallas_call(functools.partial(kernel, G, C, D, BLK), out_shape=jax.Sha...  31.8 us
    unnamed x1, local copies, waits for them, and re-layouts  1.28 us

profile of v4, /device:TPU:1, one launch (start us, length us, event | category | flops | bytes accessed | tf_op | source)
XLA Modules:
  0.0 33.0 jit_solution(10457201297584453333)
XLA Ops:
  0.0 31.8 %shard_map.109 = bf16[2,8,128]{2,1,0:T(8,128)(2,1)} custom-call(bf16[2,8,4096]{2,1,0:T(8,128)(2,1)} %hidden_h.1, bf16[8,512,1024]{2,1,0:T(8,128)(2,1)} %cache_h.1, s32[32]{0:T(128)} %lengths_h.1, s32[12]{0:T(128)} %source_h.1, s32[12]{0:T(128)} %target_h.1, bf16[4096,256]{1,0:T(8,128)(2,1)} %wq_h.1, bf16[32,4096]{1,0:T(8,128)(2,1)} %bitcast.1, ...), custom_call_target="tpu_custom_call" | custom-call | tf_op jit(solution)/shard_map/pallas_call | solution.py:411
  31.8 1.3 %copy.13 = bf16[2,8,128]{2,1,0:T(8,128)(2,1)} copy(bf16[2,8,128]{2,1,0:T(8,128)(2,1)} %shard_map.109) | data formatting | bytes 8192

commit v5 on v4

--- a/solution.py
+++ b/solution.py
@@ -53,7 +53,7 @@
     hidden_h, cache_h, lengths_h, source_h, target_h, wq_h, wkv_h, qgain_h, kgain_h, wo_h, freq_h,
     out_ref,
     hidden, cache, wq, wkv, wo, qgain, kgain, freq, lengths, source, target,
-    raw, z_send, z_recv, pre, q_early, q_late, kv_pre, kv_send, kv_recv, a_send, a_recv, ml_send, ml_recv, mix,
+    raw, z_send, z_recv, pre, q_early, q_late, turned_keys, kv_pre, kv_send, kv_recv, a_send, a_recv, ml_send, ml_recv, mix,
     o_send, o_recv, y_send, y_recv,
     load_sem, zs_sem, zr_sem, qs_sem, qr_sem, ks_sem, kr_sem, as_sem, ar_sem, ms_sem, mr_sem,
     os_sem, or_sem, ys_sem, yr_sem,
@@ -96,9 +96,11 @@
     copies += [(lengths_h, lengths), (freq_h, freq), (qgain_h, qgain), (kgain_h, kgain)]
     copies += [(cache_h, cache), (wo_h, wo)]
     loads = [pltpu.make_async_copy(a, b, load_sem.at[n]) for n, (a, b) in enumerate(copies)]
-    for load in loads[:-2]:
+    for load in loads[:3]:
         load.start()
     lax.fori_loop(0, C - 1, greet, 0)
+    for load in loads[3:-2]:
+        load.start()
 
     for load in loads[3:-2]:
         load.wait()
@@ -121,18 +123,6 @@
         count = count + jnp.where(listed[r], 0, 1)
     row_lengths = [lengths[my_g * ROWS + order[r]] for r in range(ROWS)]
 
-    at, lane = iota((RQ + SR, HEAD_DIM), 0), iota((RQ + SR, HEAD_DIM), 1)
-    row = jnp.where(at < RQ, at >> 2, (at - RQ) >> 1)
-    position = at & 1
-    for r in range(ROWS):
-        position = position + jnp.where(row == r, row_lengths[r], 0)
-    angle = position.astype(F32) * freq[...]
-    cos = jnp.cos(angle)
-    sin = jnp.sin(angle)
-    sin = jnp.where(lane < HEAD_DIM // 2, -sin, sin)
-    q_gain = qgain[...].astype(F32).reshape(1, HEAD_DIM) * QSCALE
-    k_gain = kgain[...].astype(F32).reshape(1, HEAD_DIM)
-
     loads[1].wait()
     loads[2].wait()
     h = jnp.concatenate([hidden[0], hidden[1]], axis=0)
@@ -156,6 +146,18 @@
         remote(z_send.at[n], z_recv.at[n], zs_sem, zr_sem, group=(my_g + n + 1) & (G - 1)).start()
     drains.append(lambda: bytes_of(z_send, zs_sem))
 
+    at, lane = iota((RQ + SR, HEAD_DIM), 0), iota((RQ + SR, HEAD_DIM), 1)
+    row = jnp.where(at < RQ, at >> 2, (at - RQ) >> 1)
+    position = at & 1
+    for r in range(ROWS):
+        position = position + jnp.where(row == r, row_lengths[r], 0)
+    angle = position.astype(F32) * freq[...]
+    cos = jnp.cos(angle)
+    sin = jnp.sin(angle)
+    sin = jnp.where(lane < HEAD_DIM // 2, -sin, sin)
+    q_gain = qgain[...].astype(F32).reshape(1, HEAD_DIM) * QSCALE
+    k_gain = kgain[...].astype(F32).reshape(1, HEAD_DIM)
+
     def send_queries(half):
         rows = slice(half * HALF, (half + 1) * HALF)
         turned = rotated(normed(pre[rows, :], q_gain), cos[rows], sin[rows]).astype(BF16)
@@ -229,6 +231,16 @@
     place = iota((2 * M, BLK), 1) + my_c * BLK
     lanes = iota((2 * M, HEAD_DIM), 1) - (iota((2 * M, HEAD_DIM), 0) & 3)
     loads[-2].wait()
+
+    PAIR = 2 * HEAD_DIM
+    unit = (iota((PAIR, PAIR), 0) == iota((PAIR, PAIR), 1)).astype(F32).astype(BF16)
+    for n, r in enumerate(halves[1]):
+        for k in range(KV_HEADS // 2):
+            at = slice(k * PAIR, (k + 1) * PAIR)
+            x = lax.dot_general(
+                unit, cache[order[r], :, at], (((1,), (1,)), ((), ())), preferred_element_type=F32
+            )
+            turned_keys[n, at, :] = x.astype(BF16)
 
     def attend(half):
         rows = halves[half]
@@ -251,9 +263,12 @@
                 both = jnp.concatenate(
                     [jnp.concatenate([a, blank], axis=1), jnp.concatenate([blank, b], axis=1)], axis=0
                 )
-                x = lax.dot_general(
-                    both, cache[order[r], :, k_at], (((1,), (1,)), ((), ())), preferred_element_type=F32
-                )
+                if half:
+                    x = jnp.dot(both, turned_keys[n, k_at, :], preferred_element_type=F32)
+                else:
+                    x = lax.dot_general(
+                        both, cache[order[r], :, k_at], (((1,), (1,)), ((), ())), preferred_element_type=F32
+                    )
                 scores.append(jnp.where(place < row_lengths[r], x, FLOOR))
             for x in scores:
                 peaks.append(jnp.maximum(jnp.max(x, axis=1, keepdims=True), LOW).astype(BF16).astype(F32))
@@ -289,7 +304,10 @@
                 return carry
 
             if half:
-                for n in range(2 * JJ - i):
+                turns = range(2 * JJ - i)
+                if JJ == 8:
+                    turns = (0, 1, 8, 9, 2, 3, 4, 5, 10, 11, 12, 13, 6, 7, 14, 15)[: 2 * JJ - i]
+                for n in turns:
                     send_to(n, 0)
             else:
                 lax.fori_loop(0, 2 * JJ - i, send_to, 0)
@@ -363,8 +381,16 @@
         ).astype(BF16)
         for n in range(JJ):
             o_send[g * JJ + n] = part[:, n * width : (n + 1) * width]
-        for n in range(JJ - (FAR_FIRST[i] == 0)):
-            dest = neighbour(g, n)
+        if i == 1:
+            turns = [(0, n) for n in range(JJ)] + [(1, n) for n in range(JJ)]
+        elif i == 3:
+            turns = [(2, n) for n in range(JJ)] + [(3, n) for n in range(JJ - 1)]
+            if JJ == 8:
+                turns = [turns[n] for n in (0, 1, 8, 9, 2, 3, 4, 5, 10, 11, 12, 13, 6, 7, 14)]
+        else:
+            turns = []
+        for a, n in turns:
+            dest = neighbour(my_x ^ FAR_FIRST[a], n)
             remote(o_send.at[dest], o_recv.at[my_c], os_sem, or_sem, ctx=dest).start()
     drains.append(lambda: bytes_of(o_send.at[pl.ds(0, C - 1)], os_sem))
     o_recv[my_c] = o_send[my_c]
@@ -422,6 +448,7 @@
             pltpu.VMEM((RQ, HEAD_DIM), F32),
             pltpu.VMEM((C, HALF, HEAD_DIM), BF16),
             pltpu.VMEM((C, HALF, HEAD_DIM), BF16),
+            pltpu.VMEM((ROWS // 2, KV_HEADS * HEAD_DIM, BLK), BF16),
             pltpu.VMEM((SR, HEAD_DIM), F32),
             pltpu.VMEM((SR, HEAD_DIM), BF16),
             pltpu.VMEM((max(2 * pieces, JJ), SR, HEAD_DIM), BF16),

time: 33.2 us -> 33.1 us (level)
  no operation moved by 1% of the time
where the time goes in v5:
time: 33.1 us; the launch traced here: 32.9 us
  Pallas kernels  31.6 us (95%)
  local copies, waits for them, and re-layouts  1.28 us (4%)
    pallas_call x1, Pallas kernels, per_device(): pl.pallas_call(functools.partial(kernel, G, C, D, BLK), out_shape=jax.Sha...  31.6 us
    unnamed x1, local copies, waits for them, and re-layouts  1.28 us

profile of v5, /device:TPU:1, one launch (start us, length us, event | category | flops | bytes accessed | tf_op | source)
XLA Modules:
  0.0 32.9 jit_solution(18087062757228372890)
XLA Ops:
  0.0 31.6 %shard_map.109 = bf16[2,8,128]{2,1,0:T(8,128)(2,1)} custom-call(bf16[2,8,4096]{2,1,0:T(8,128)(2,1)} %hidden_h.1, bf16[8,512,1024]{2,1,0:T(8,128)(2,1)} %cache_h.1, s32[32]{0:T(128)} %lengths_h.1, s32[12]{0:T(128)} %source_h.1, s32[12]{0:T(128)} %target_h.1, bf16[4096,256]{1,0:T(8,128)(2,1)} %wq_h.1, bf16[32,4096]{1,0:T(8,128)(2,1)} %bitcast.1, ...), custom_call_target="tpu_custom_call" | custom-call | tf_op jit(solution)/shard_map/pallas_call | solution.py:437
  31.6 1.3 %copy.13 = bf16[2,8,128]{2,1,0:T(8,128)(2,1)} copy(bf16[2,8,128]{2,1,0:T(8,128)(2,1)} %shard_map.109) | data formatting | bytes 8192

commit v6 on v5

--- a/solution.py
+++ b/solution.py
@@ -53,7 +53,7 @@
     hidden_h, cache_h, lengths_h, source_h, target_h, wq_h, wkv_h, qgain_h, kgain_h, wo_h, freq_h,
     out_ref,
     hidden, cache, wq, wkv, wo, qgain, kgain, freq, lengths, source, target,
-    raw, z_send, z_recv, pre, q_early, q_late, turned_keys, kv_pre, kv_send, kv_recv, a_send, a_recv, ml_send, ml_recv, mix,
+    raw, z_send, z_recv, pre, q_early, q_late, turned_keys, kv_pre, kv_send, kv_recv, a_send, a_recv, ml_send, ml_recv, spread, mix,
     o_send, o_recv, y_send, y_recv,
     load_sem, zs_sem, zr_sem, qs_sem, qr_sem, ks_sem, kr_sem, as_sem, ar_sem, ms_sem, mr_sem,
     os_sem, or_sem, ys_sem, yr_sem,
@@ -297,9 +297,9 @@
 
             def send_to(n, carry):
                 dest = neighbour(jnp.where((n >= JJ) == (i == 1), last, nearer), n & (JJ - 1))
-                remote(send.at[dest], recv.at[my_c], as_sem, ar_sem, ctx=dest).start()
                 if half:
                     remote(ml_send.at[dest], ml_recv.at[my_c], ms_sem, mr_sem, ctx=dest).start()
+                remote(send.at[dest], recv.at[my_c], as_sem, ar_sem, ctx=dest).start()
 
                 return carry
 
@@ -355,12 +355,14 @@
     scale = jnp.exp2(peaks - highest)
     new_scale = jnp.exp2(new_peak - highest)
     norm = jnp.sum(scale * totals, axis=1, keepdims=True) + new_scale * new_total
+    for n in range(C):
+        spread[n] = jnp.broadcast_to(scale[:, n : n + 1], (RQ, HEAD_DIM))
     bytes_of(a_recv.at[:, pl.ds(0, C - 1)], ar_sem)
     for half in range(2):
         rows = slice(half * HALF, (half + 1) * HALF)
         acc = [(new_sums * new_scale)[rows]] + [jnp.zeros((HALF, HEAD_DIM), F32)] * 3
         for n in range(C):
-            acc[n & 3] = acc[n & 3] + a_recv[half, n].astype(F32) * scale[rows, n : n + 1]
+            acc[n & 3] = acc[n & 3] + a_recv[half, n].astype(F32) * spread[n, rows, :]
         mix[rows, :] = ((acc[0] + acc[1]) + (acc[2] + acc[3])) / norm[rows]
     mixed = jnp.concatenate(
         [
@@ -456,6 +458,7 @@
             pltpu.VMEM((2, C, HALF, HEAD_DIM), BF16),
             pltpu.VMEM((C, 1, HEAD_DIM), F32),
             pltpu.VMEM((C, 1, HEAD_DIM), F32),
+            pltpu.VMEM((C, RQ, HEAD_DIM), F32),
             pltpu.VMEM((RQ, HEAD_DIM), F32),
             pltpu.VMEM((C, SR, D // C), BF16),
             pltpu.VMEM((C, SR, D // C), BF16),

time: 33.1 us -> 33 us (level)
  no operation moved by 1% of the time
where the time goes in v6:
time: 33 us; the launch traced here: 32.8 us
  Pallas kernels  31.5 us (95%)
  local copies, waits for them, and re-layouts  1.28 us (4%)
    pallas_call x1, Pallas kernels, per_device(): pl.pallas_call(functools.partial(kernel, G, C, D, BLK), out_shape=jax.Sha...  31.5 us
    unnamed x1, local copies, waits for them, and re-layouts  1.28 us

profile of v6, /device:TPU:1, one launch (start us, length us, event | category | flops | bytes accessed | tf_op | source)
XLA Modules:
  0.0 32.8 jit_solution(15882149906871114732)
XLA Ops:
  0.0 31.5 %shard_map.109 = bf16[2,8,128]{2,1,0:T(8,128)(2,1)} custom-call(bf16[2,8,4096]{2,1,0:T(8,128)(2,1)} %hidden_h.1, bf16[8,512,1024]{2,1,0:T(8,128)(2,1)} %cache_h.1, s32[32]{0:T(128)} %lengths_h.1, s32[12]{0:T(128)} %source_h.1, s32[12]{0:T(128)} %target_h.1, bf16[4096,256]{1,0:T(8,128)(2,1)} %wq_h.1, bf16[32,4096]{1,0:T(8,128)(2,1)} %bitcast.1, ...), custom_call_target="tpu_custom_call" | custom-call | tf_op jit(solution)/shard_map/pallas_call | solution.py:439
  31.6 1.3 %copy.13 = bf16[2,8,128]{2,1,0:T(8,128)(2,1)} copy(bf16[2,8,128]{2,1,0:T(8,128)(2,1)} %shard_map.109) | data formatting | bytes 8192
